TPU v7x, 32 devices: a whole 2x2x4 slice. The times are simulated.
32 devices in a mesh: grp: 4 (over y, core), feat: 8 (over z, x).
Axes of the slice: x: 2, y: 2, z: 4, core: 2. Of those that a mesh axis runs over, the one named last changes fastest.
Arguments:
- features: bfloat16 [128, 16384], P('feat', 'grp'), may hold values from -6 to 6
- w_self: bfloat16 [128, 256], replicated, may hold values from -0.5 to 0.5
- w_neigh: bfloat16 [128, 256], replicated, may hold values from -0.5 to 0.5
- bias: float32 [256], replicated, may hold values from -3 to 3
- tile_vals: bfloat16 [4, 8, 8, 128, 128], P('grp'), may hold values from -0.5 to 0.5
- tile_src: int32 [4, 8, 8], P('grp'), may hold values from 0 to 39, as said below
- tile_dst: int32 [4, 8, 8], P('grp'), may hold values from 0 to 3
- tile_count: int32 [4, 8], P('grp'), may hold values from 1 to 8, as said below
- hub_blocks: int32 [4, 2], P('grp'), may hold values from 0 to 31, as said below
- cotangent: bfloat16 [16384, 256], P(('grp', 'feat')), may hold values from -6 to 6
Outputs:
- output: bfloat16 [16384, 256], P(('grp', 'feat'))
- feat_grad: float32 [128, 16384], P('feat', 'grp')
- wself_grad: float32 [128, 256], P('feat')
- wneigh_grad: float32 [128, 256], P('feat')
- bias_grad: float32 [256], replicated
Inputs may be any that keep to these rules, and one draw needn't show every extreme that they name: `tile_src`: a slot number of the tile's own group's blocks below 32, or 32 plus a hub number. `tile_count`: some owner uses all 8 slots in every draw. `hub_blocks`: the 2 block numbers of a group are distinct.
All inputs are finite; a program needn't handle non-finite values.
Results may differ from a plain program's by a relative error of at most 0.0055.
Values may be sent and summed in bfloat16 or wider, within the bound.
A program may use at most 128 MiB of HBM per device.

v0:
```python
import jax
import jax.numpy as jnp
from jax import lax
from jax.sharding import PartitionSpec as P


def silu_parts(preact):
    sig = jax.nn.sigmoid(preact)
    return (preact * sig, sig * (1.0 + preact * (1.0 - sig)))


def contract_first(left, right):
    return lax.dot_general(
        left, right, (((0,), (0,)), ((), ())), preferred_element_type=jnp.float32
    )


def contract_last(left, right):
    return lax.dot_general(
        left, right, (((1,), (1,)), ((), ())), preferred_element_type=jnp.float32
    )


def local(
    features,
    w_self,
    w_neigh,
    bias,
    tile_vals,
    tile_src,
    tile_dst,
    tile_count,
    hub_blocks,
    cotangent,
):
    columns, group_nodes = features.shape
    owners = lax.axis_size("feat")
    position = lax.axis_index("feat")
    slot_count = tile_src.shape[2]
    tile_size = tile_vals.shape[-1]
    group_blocks = group_nodes // tile_size
    own_blocks = group_blocks // owners
    row_count = own_blocks * tile_size
    hub_ids = hub_blocks[0]
    highest = lax.Precision.HIGHEST
    own_hubs = jnp.take(
        features.reshape(columns, group_blocks, tile_size), hub_ids, axis=1
    ).reshape(columns, -1)
    all_hubs = lax.all_gather(own_hubs, "grp", axis=1, tiled=True)
    slot_total = group_blocks + all_hubs.shape[1] // tile_size
    upstream = cotangent.astype(jnp.float32)
    combined = jnp.concatenate([features, all_hubs], axis=1)
    full = lax.all_gather(combined, "feat", axis=0, tiled=True)
    feat_total = full.shape[0]
    values = lax.dynamic_index_in_dim(tile_vals[0], position, 0, keepdims=False)
    src_ids = lax.dynamic_index_in_dim(tile_src[0], position, 0, keepdims=False)
    dst_ids = lax.dynamic_index_in_dim(tile_dst[0], position, 0, keepdims=False)
    live_count = lax.dynamic_index_in_dim(tile_count[0], position, 0, keepdims=False)
    live_slots = (jnp.arange(slot_count, dtype=jnp.int32) < live_count).astype(jnp.float32)
    picked = jnp.take(full.reshape(feat_total, slot_total, tile_size), src_ids, axis=1)
    contrib = (
        jnp.einsum("tds,fts->ftd", values, picked, preferred_element_type=jnp.float32)
        * live_slots[None, :, None]
    )
    dst_hot = (dst_ids[:, None] == jnp.arange(own_blocks, dtype=jnp.int32)[None, :]).astype(
        jnp.float32
    )
    agg_own = (
        jnp.einsum("ftd,tb->fbd", contrib, dst_hot, precision=highest)
        .reshape(feat_total, row_count)
        .astype(jnp.bfloat16)
    )
    feat_own = lax.dynamic_slice_in_dim(full, position * row_count, row_count, 1)
    preact = contract_first(feat_own, w_self) + contract_first(agg_own, w_neigh) + bias
    activated, slope = silu_parts(preact)
    output = activated.astype(jnp.bfloat16)
    grad_pre = (upstream * slope).astype(jnp.bfloat16)
    wself_full = jnp.dot(feat_own, grad_pre, preferred_element_type=jnp.float32)
    wneigh_full = jnp.dot(agg_own, grad_pre, preferred_element_type=jnp.float32)
    bias_grad = jnp.sum(grad_pre.astype(jnp.float32), axis=0)
    wself_full, wneigh_full, bias_grad = lax.psum(
        (wself_full, wneigh_full, bias_grad), ("grp", "feat")
    )
    wself_grad = lax.dynamic_slice_in_dim(wself_full, position * columns, columns, 0)
    wneigh_grad = lax.dynamic_slice_in_dim(wneigh_full, position * columns, columns, 0)
    self_grad = contract_last(w_self, grad_pre)
    agg_grad = contract_last(w_neigh, grad_pre).astype(jnp.bfloat16)
    chosen = jnp.take(agg_grad.reshape(feat_total, own_blocks, tile_size), dst_ids, axis=1)
    src_grad = (
        jnp.einsum("tds,ftd->fts", values, chosen, preferred_element_type=jnp.float32)
        * live_slots[None, :, None]
    )
    src_hot = (src_ids[:, None] == jnp.arange(slot_total, dtype=jnp.int32)[None, :]).astype(
        jnp.float32
    )
    slot_grad = jnp.einsum("fts,tk->fks", src_grad, src_hot, precision=highest).reshape(
        feat_total, slot_total * tile_size
    )
    own_part = lax.dynamic_slice_in_dim(slot_grad, position * row_count, row_count, 1) + self_grad
    slot_grad = lax.dynamic_update_slice_in_dim(slot_grad, own_part, position * row_count, 1)
    mine = lax.psum_scatter(slot_grad, "feat", scatter_dimension=0, tiled=True)
    local_grad = mine[:, :group_nodes]
    hub_part = mine[:, group_nodes:]
    hub_back = (
        lax.psum_scatter(hub_part.astype(jnp.bfloat16), "grp", scatter_dimension=1, tiled=True)
        .astype(jnp.float32)
        .reshape(columns, -1, tile_size)
    )
    local_blocks = local_grad.reshape(columns, group_blocks, tile_size).at[:, hub_ids].add(hub_back)
    feat_grad = local_blocks.reshape(columns, group_nodes)
    return (output, feat_grad, wself_grad, wneigh_grad, bias_grad)


def solution(mesh):
    return jax.shard_map(
        local,
        mesh=mesh,
        in_specs=(
            P("feat", "grp"),
            P(),
            P(),
            P(),
            P("grp", None, None, None, None),
            P("grp", None, None),
            P("grp", None, None),
            P("grp", None),
            P("grp", None),
            P(("grp", "feat"), None),
        ),
        out_specs=(
            P(("grp", "feat"), None),
            P("feat", "grp"),
            P("feat", None),
            P("feat", None),
            P(),
        ),
        check_vma=False,
    )
```

profile of v0, /device:TPU:0, one launch (start us, length us, event | category | flops | bytes accessed | tf_op | source)
XLA Modules:
  0.0 304.6 jit_solution(11308443132222153842)
XLA Ops:
  7.2 0.0 all-gather.2.cloned.1.call-start
  7.2 0.8 fusion.38
  8.0 0.7 compare_and_fusion.2
  8.7 0.1 broadcast_bitcast_fusion
  8.8 0.9 copy_bitcast_fusion.3
  9.7 0.6 gather_fusion
  10.3 6.2 %all_gather.6 = bf16[16,1024]{1,0:T(8,128)(2,1)S(1)} all-gather(bf16[16,256]{1,0:T(8,128)(2,1)S(1)} %bitcast_select_fusion), channel_id=1, replica_groups=mesh['grp'=4,'feat'=8] {'grp'}, dimensions={1}, use_global_device_ids=true | all-gather | bytes 40960 | tf_op jit(solution)/shard_map/all_gather | solution.py:49
  16.5 1.6 pad_maximum_fusion
  18.1 0.0 all-reduce.3.cloned.1.call-start
  18.2 1.2 constant_dynamic-slice_fusion.3
  19.4 0.6 compare_convert_fusion
  20.1 0.7 fusion.39
  20.8 0.7 fusion.40
  21.5 0.7 compare_and_fusion
  22.2 39.8 %all-gather.2.cloned.1.call-done = bf16[128,5120]{1,0:T(8,128)(2,1)} async-done(((bf16[16,5120]{1,0:T(8,128)(2,1)}), bf16[128,5120]{1,0:T(8,128)(2,1)}) %all-gather.2.cloned.1.call-update) | async-done | bytes 1310736 | tf_op jit(solution)/shard_map/all_gather | solution.py:53
  62.0 1.8 copy.37
  63.8 1.4 copy.38
  65.2 2.0 gather_fusion.1
  67.2 0.4 fusion.1
  67.5 0.7 convolution_convert_fusion.1
  68.2 1.2 fusion.26
  69.4 1.2 convert_reduce_fusion
  70.6 0.9 fusion.17
  71.4 0.2 convolution_convert_fusion
  71.7 0.1 copy.40
  71.8 0.6 gather_fusion.2
  72.4 0.3 fusion
  72.7 1.3 fusion.4
  74.0 0.5 copy.73
  74.5 1.5 copy-done.1
  76.0 0.1 copy.47
  76.1 1.8 fusion.24
  77.9 0.0 reduce-scatter.3.cloned.1.call-start
  78.0 0.2 fusion.3
  78.2 0.1 copy.43
  78.3 0.8 constant_dynamic-update-slice_fusion
  79.1 0.0 reduce-scatter.5.cloned.1.call-start
  79.2 39.1 %psum.23 = f32[256]{0:T(256)} all-reduce(f32[256]{0:T(256)S(1)} %get-tuple-element.7), channel_id=1, replica_groups=mesh['grp'=4,'feat'=8] {'grp','feat'}, use_global_device_ids=true, to_apply=%region_6.7 | all-reduce | flops 256 | bytes 2048 | tf_op jit(solution)/shard_map/psum | solution.py:81
  118.2 83.7 %all-reduce.3.cloned.1.call-done = (f32[128,256]{1,0:T(8,128)}, f32[128,256]{1,0:T(8,128)}) async-done(((f32[128,256]{1,0:T(8,128)}, f32[128,256]{1,0:T(8,128)}), (f32[128,256]{1,0:T(8,128)}, f32[128,256]{1,0:T(8,128)})) %all-reduce.3.cloned.1.call-update) | async-done | bytes 262160 | tf_op jit(solution)/shard_map/psum | solution.py:81
  201.9 1.3 constant_dynamic-slice_fusion.1
  203.2 1.3 constant_dynamic-slice_fusion
  204.6 70.2 %reduce-scatter.3.cloned.1.call-done = f32[16,5120]{1,0:T(8,128)} async-done(((f32[128,5120]{1,0:T(8,128)}), f32[16,5120]{1,0:T(8,128)}) %reduce-scatter.3.cloned.1.call-update) | async-done | bytes 327696 | tf_op jit(solution)/shard_map/reduce_scatter | solution.py:101
  274.8 1.5 slice.19
  276.3 1.0 copy_bitcast_fusion.2
  277.3 18.7 %reduce-scatter.5.cloned.1.call-done = bf16[16,256]{1,0:T(8,128)(2,1)} async-done(((bf16[16,1024]{1,0:T(8,128)(2,1)}), bf16[16,256]{1,0:T(8,128)(2,1)}) %reduce-scatter.5.cloned.1.call-update) | async-done | bytes 8208 | tf_op jit(solution)/shard_map/reduce_scatter | solution.py:105
  296.0 0.7 reshape.194
  296.7 0.6 scatter_fusion
  297.3 0.7 copy_bitcast_fusion.1
  (21 shorter events, 0.1 us)
Async XLA Ops:
  7.2 60.0 %copy-start = (bf16[1,8,8,128,128]{4,3,2,1,0:T(8,128)(2,1)S(1)}, bf16[1,8,8,128,128]{4,3,2,1,0:T(8,128)(2,1)}, u32[]{:S(2)}) copy-start(bf16[1,8,8,128,128]{4,3,2,1,0:T(8,128)(2,1)} %param.14) | copy-start | bytes 6291460
  7.2 54.8 %all-gather.2.cloned.1.call-start = ((), (), s32[]{:S(2)}) async-start(), calls=%async_computation.2 | async-start | bytes 1474560 | tf_op jit(solution)/shard_map/all_gather | solution.py:53
  18.1 183.8 %all-reduce.3.cloned.1.call-start = ((), (), s32[]{:S(2)}) async-start(), calls=%async_computation.5 | async-start | bytes 524288 | tf_op jit(solution)/shard_map/psum | solution.py:81
  63.8 4.5 %copy-start.2 = (bf16[128,256]{1,0:T(8,128)(2,1)S(1)}, bf16[128,256]{1,0:T(8,128)(2,1)}, u32[]{:S(2)}) copy-start(bf16[128,256]{1,0:T(8,128)(2,1)} %param.11) | copy-start | bytes 196612
  65.2 4.2 %copy-start.3 = (bf16[128,256]{1,0:T(8,128)(2,1)S(1)}, bf16[128,256]{1,0:T(8,128)(2,1)}, u32[]{:S(2)}) copy-start(bf16[128,256]{1,0:T(8,128)(2,1)} %param.12) | copy-start | bytes 196612
  65.2 4.2 %copy-start.4 = (bf16[512,256]{1,0:T(8,128)(2,1)S(1)}, bf16[512,256]{1,0:T(8,128)(2,1)}, u32[]{:S(2)}) copy-start(bf16[512,256]{1,0:T(8,128)(2,1)} %param.19) | copy-start | bytes 786436
  65.2 4.2 %copy-start.5 = (f32[256]{0:T(256)S(1)}, f32[256]{0:T(256)}, u32[]{:S(2)}) copy-start(f32[256]{0:T(256)} %param.13) | copy-start | bytes 3076
  74.5 1.5 copy-start.1
  77.9 196.9 %reduce-scatter.3.cloned.1.call-start = ((), (), s32[]{:S(2)}) async-start(), calls=%async_computation.3 | async-start | bytes 2949120 | tf_op jit(solution)/shard_map/reduce_scatter | solution.py:101
  79.1 216.9 %reduce-scatter.5.cloned.1.call-start = ((), (), s32[]{:S(2)}) async-start(), calls=%async_computation.4 | async-start | bytes 40960 | tf_op jit(solution)/shard_map/reduce_scatter | solution.py:105
Sparse Core Ops, SparseCore 0:
  18.2 43.7 all-gather.1
  78.0 123.8 all-reduce.2
  205.4 69.3 reduce-scatter.2
  277.6 18.3 reduce-scatter.4
where the time goes:
time: 305 us
  waiting for transfers between devices  213 us (70%)
  blocking collectives  45.3 us (15%)
  local copies, waits for them, and re-layouts  18.2 us (6%)
  between operations  14 us (5%)
  matrix products  7.97 us (3%)
  other arithmetic  6.42 us (2%)
    psum x1, waiting for transfers between devices, local(): lax.psum((wself_full, wneigh_full, bias_grad), ('grp', 'feat'))  83.7 us
    reduce_scatter x1, waiting for transfers between devices, local(): mine = lax.psum_scatter(slot_grad, 'feat', scatter_dimension=0, tiled=True)  70.2 us
    all_gather x1, waiting for transfers between devices, local(): full = lax.all_gather(combined, 'feat', axis=0, tiled=True)  39.8 us
    psum x1, blocking collectives, local(): lax.psum((wself_full, wneigh_full, bias_grad), ('grp', 'feat'))  39.1 us
    reduce_scatter x1, waiting for transfers between devices, local(): lax.psum_scatter(hub_part.astype(jnp.bfloat16), 'grp', scatter_dimension=...  18.7 us
    all_gather x1, blocking collectives, local(): all_hubs = lax.all_gather(own_hubs, 'grp', axis=1, tiled=True)  6.23 us
  transfers between devices with their start and end apart: 4, of which 4 were waited for; matrix products, arithmetic and copies ran while one was open for 3% of the time, Pallas kernels for 0%

commit v1 on v0

v1 whole, which is shorter than its diff:
```python
import functools

import jax
import jax.numpy as jnp
from jax import lax
from jax.experimental import pallas as pl
from jax.experimental.pallas import tpu as pltpu
from jax.sharding import PartitionSpec as P


def lanes(index, width):
    return pl.ds(pl.multiple_of(index * width, width), width)


def gather_tiles(own_blocks, src_ref, dst_ref, x_ref, tiles_ref, out_ref):
    owners, slots, size, _ = tiles_ref.shape
    rows = x_ref.shape[0]

    def owner(o, carry):
        total = jnp.zeros((own_blocks * rows, size), jnp.float32)
        for t in range(slots):
            x = x_ref[:, lanes(src_ref[o * slots + t], size)].astype(jnp.float32)
            dst = dst_ref[o * slots + t]
            left = jnp.concatenate(
                [x * (dst == d).astype(jnp.float32) for d in range(own_blocks)], axis=0
            ).astype(jnp.bfloat16)
            total += lax.dot_general(
                left, tiles_ref[o, t], (((1,), (1,)), ((), ())), preferred_element_type=jnp.float32
            )
        for d in range(own_blocks):
            out_ref[:, lanes(o * own_blocks + d, size)] = total[d * rows : (d + 1) * rows].astype(
                out_ref.dtype
            )
        return carry

    lax.fori_loop(0, owners, owner, 0)


def scatter_tiles(own_blocks, src_ref, dst_ref, g_ref, tiles_ref, self_ref, out_ref, hub_ref, total):
    owners, slots, size, _ = tiles_ref.shape
    nodes = g_ref.shape[1]
    total[:, :nodes] = self_ref[...].astype(jnp.float32)
    total[:, nodes:] = jnp.zeros((total.shape[0], total.shape[1] - nodes), jnp.float32)

    def owner(o, carry):
        terms = []
        for t in range(slots):
            dst = dst_ref[o * slots + t]
            g = g_ref[:, lanes(o * own_blocks + jnp.maximum(dst, 0), size)]
            term = jnp.dot(g, tiles_ref[o, t], preferred_element_type=jnp.float32)
            terms.append(term * (dst >= 0).astype(jnp.float32))
        for t in range(slots):
            at = lanes(src_ref[o * slots + t], size)
            total[:, at] = total[:, at] + terms[t]
        return carry

    lax.fori_loop(0, owners, owner, 0)
    out_ref[...] = total[:, :nodes]
    hub_ref[...] = total[:, nodes:].astype(hub_ref.dtype)


def add_hubs(ids_ref, part_ref, hub_ref, out_ref):
    peers, _, width = hub_ref.shape
    hubs = ids_ref.shape[0]
    size = width // hubs
    out_ref[...] = part_ref[...]
    back = hub_ref[0].astype(jnp.float32)
    for p in range(1, peers):
        back += hub_ref[p].astype(jnp.float32)
    for k in range(hubs):
        at = lanes(ids_ref[k], size)
        out_ref[:, at] = out_ref[:, at] + back[:, k * size : (k + 1) * size]


def local(
    features,
    w_self,
    w_neigh,
    bias,
    tile_vals,
    tile_src,
    tile_dst,
    tile_count,
    hub_blocks,
    cotangent,
):
    columns, nodes = features.shape
    owners = lax.axis_size("feat")
    position = lax.axis_index("feat")
    size = tile_vals.shape[-1]
    slots = tile_src.shape[2]
    own_blocks = nodes // size // owners
    hubs = hub_blocks.shape[1]
    rows = max(columns, 16)
    vmem, smem = pl.BlockSpec(memory_space=pltpu.VMEM), pl.BlockSpec(memory_space=pltpu.SMEM)
    params = pltpu.CompilerParams(vmem_limit_bytes=40 * 1024 * 1024)

    def padded(a):
        return a if rows == columns else jnp.pad(a, ((0, rows - columns), (0, 0)))

    own_hubs = jnp.concatenate(
        [lax.dynamic_slice_in_dim(features, hub_blocks[0, k] * size, size, 1) for k in range(hubs)],
        axis=1,
    )
    all_hubs = lax.all_gather(own_hubs, "grp", axis=1, tiled=True)
    combined = padded(jnp.concatenate([features, all_hubs], axis=1))
    live = jnp.arange(slots, dtype=jnp.int32)[None, :] < tile_count[0][:, None]
    src = tile_src[0].reshape(-1)
    dst = jnp.where(live, tile_dst[0], -1).reshape(-1)
    tiles = tile_vals[0]
    agg = pl.pallas_call(
        functools.partial(gather_tiles, own_blocks),
        out_shape=jax.ShapeDtypeStruct((rows, nodes), jnp.bfloat16),
        in_specs=[smem, smem, vmem, vmem],
        out_specs=vmem,
        compiler_params=params,
        name="gather_tiles",
    )(src, dst, combined, tiles)[:columns]
    both = lax.all_to_all(
        jnp.stack([features, agg]), "feat", split_axis=2, concat_axis=1, tiled=True
    )
    both = both.reshape(-1, both.shape[2])
    weights = jnp.concatenate([w_self, w_neigh], axis=0)
    preact = (
        lax.dot_general(both, weights, (((0,), (0,)), ((), ())), preferred_element_type=jnp.float32)
        + bias
    )
    sig = jax.nn.sigmoid(preact)
    output = (preact * sig).astype(jnp.bfloat16)
    slope = sig * (1.0 + preact * (1.0 - sig))
    grad_pre = (cotangent.astype(jnp.float32) * slope).astype(jnp.bfloat16)
    grads = lax.dot_general(
        weights, grad_pre, (((1,), (1,)), ((), ())), preferred_element_type=jnp.float32
    ).astype(jnp.bfloat16)
    back = lax.all_to_all(
        grads.reshape(2, -1, grads.shape[1]), "feat", split_axis=1, concat_axis=2, tiled=True
    )
    weight_part = jnp.dot(both, grad_pre, preferred_element_type=jnp.float32)
    bias_part = jnp.sum(grad_pre.astype(jnp.float32), axis=0)
    weight_sum, bias_grad = lax.psum((weight_part, bias_part), ("grp", "feat"))
    weight_sum = lax.dynamic_slice_in_dim(
        weight_sum.reshape(2, -1, weight_sum.shape[1]), position * columns, columns, 1
    )
    part, hub_part = pl.pallas_call(
        functools.partial(scatter_tiles, own_blocks),
        out_shape=(
            jax.ShapeDtypeStruct((rows, nodes), jnp.float32),
            jax.ShapeDtypeStruct((rows, combined.shape[1] - nodes), jnp.bfloat16),
        ),
        in_specs=[smem, smem, vmem, vmem, vmem],
        out_specs=(vmem, vmem),
        scratch_shapes=[pltpu.VMEM((rows, combined.shape[1]), jnp.float32)],
        compiler_params=params,
        name="scatter_tiles",
    )(src, dst, padded(back[1]), tiles, padded(back[0]))
    hub_back = lax.all_to_all(
        hub_part[None, :columns], "grp", split_axis=2, concat_axis=0, tiled=True
    )
    feat_grad = pl.pallas_call(
        add_hubs,
        out_shape=jax.ShapeDtypeStruct((columns, nodes), jnp.float32),
        in_specs=[smem, vmem, vmem],
        out_specs=vmem,
        compiler_params=params,
        name="add_hubs",
    )(hub_blocks[0], part[:columns], hub_back)
    return (output, feat_grad, weight_sum[0], weight_sum[1], bias_grad)


def solution(mesh):
    return jax.shard_map(
        local,
        mesh=mesh,
        in_specs=(
            P("feat", "grp"),
            P(),
            P(),
            P(),
            P("grp", None, None, None, None),
            P("grp", None, None),
            P("grp", None, None),
            P("grp", None),
            P("grp", None),
            P(("grp", "feat"), None),
        ),
        out_specs=(
            P(("grp", "feat"), None),
            P("feat", "grp"),
            P("feat", None),
            P("feat", None),
            P(),
        ),
        check_vma=False,
    )
```

time: 305 us -> 198 us (0.65)
  waiting for transfers between devices: 213 us -> 90.3 us
  starting transfers between devices: 0.16 us -> 13.6 us
  Pallas kernels: 0 us -> 6.18 us
  matrix products: 7.97 us -> 2.33 us
    reduce_scatter x2 -> x0, waiting for transfers between devices: 89 us -> none  [the longest x1 70.2 us: local(): mine = lax.psum_scatter(slot_grad, 'feat', scatter_dimension=0, tiled=True)]
    all_gather x1 -> x0, waiting for transfers between devices: 39.8 us -> none  [local(): full = lax.all_gather(combined, 'feat', axis=0, tiled=True)]
    all_to_all x0 -> x3, starting transfers between devices: none -> 13.6 us  [the longest x1 6.21 us: local(): lax.all_to_all(jnp.stack([features, agg]), 'feat', split_axis=2, concat_a...]
    all_to_all x0 -> x3, waiting for transfers between devices: none -> 9.34 us  [the longest x1 9.34 us: local(): lax.all_to_all(jnp.stack([features, agg]), 'feat', split_axis=2, concat_a...]
    pallas_call x0 -> x3, Pallas kernels: none -> 6.18 us  [the longest x1 2.81 us: local(): pl.pallas_call(functools.partial(gather_tiles, own_blocks), out_shape=jax...]
    unnamed x14 -> x24, local copies, waits for them, and re-layouts: 2.1 us -> 7.78 us
    dot_general x10 -> x3, matrix products: 7.97 us -> 2.33 us  [the longest x1 1.14 us: local(): lax.dot_general(both, weights, (((0,), (0,)), ((), ())), preferred_elemen...]
    reshape x7 -> x1, local copies, waits for them, and re-layouts: 4.91 us -> 0.97 us  [local(): grads.reshape(2, -1, grads.shape[1])]
  transfers between devices with their start and end apart: 4 -> 4, of which waited for: 4 -> 2; matrix products, arithmetic and copies ran while one was open for 3% -> 3% of each run, Pallas kernels for 0% -> 1%
where the time goes in v1:
time: 198 us; the launch traced here: 197 us
  waiting for transfers between devices  90.3 us (46%)
  blocking collectives  47 us (24%)
  local copies, waits for them, and re-layouts  18.4 us (9%)
  between operations  15.6 us (8%)
  starting transfers between devices  13.6 us (7%)
  Pallas kernels  6.18 us (3%)
  other arithmetic  3.96 us (2%)
  matrix products  2.33 us (1%)
    psum x1, waiting for transfers between devices, local(): weight_sum, bias_grad = lax.psum((weight_part, bias_part), ('grp', 'feat'))  80.9 us
    psum x1, blocking collectives, local(): weight_sum, bias_grad = lax.psum((weight_part, bias_part), ('grp', 'feat'))  40.8 us
    all_to_all x1, waiting for transfers between devices, local(): lax.all_to_all(jnp.stack([features, agg]), 'feat', split_axis=2, concat_a...  9.34 us
    unnamed x24, local copies, waits for them, and re-layouts  7.78 us
    all_gather x1, blocking collectives, local(): all_hubs = lax.all_gather(own_hubs, 'grp', axis=1, tiled=True)  6.22 us
    all_to_all x1, starting transfers between devices, local(): lax.all_to_all(jnp.stack([features, agg]), 'feat', split_axis=2, concat_a...  6.21 us
  transfers between devices with their start and end apart: 4, of which 2 were waited for; matrix products, arithmetic and copies ran while one was open for 3% of the time, Pallas kernels for 1%

profile of v1, /device:TPU:0, one launch (start us, length us, event | category | flops | bytes accessed | tf_op | source)
XLA Modules:
  0.0 197.4 jit_solution(13493369766143271281)
XLA Ops:
  7.2 0.0 copy-start.3
  7.2 1.3 fusion.1
  9.8 0.7 constant_dynamic-slice_fusion.1
  10.5 6.2 %all_gather.3 = bf16[16,1024]{1,0:T(8,128)(2,1)S(1)} all-gather(bf16[16,256]{1,0:T(8,128)(2,1)S(1)} %pad_maximum_fusion.2), channel_id=1, replica_groups=mesh['grp'=4,'feat'=8] {'grp'}, dimensions={1}, use_global_device_ids=true | all-gather | bytes 40960 | tf_op jit(solution)/shard_map/all_gather | solution.py:105
  16.7 0.9 pad_maximum_fusion.1.x_ref
  17.7 0.7 iota_compare_fusion
  18.4 0.1 lt.32
  18.5 0.8 squeeze.23
  19.2 0.8 reshape_squeeze.3.src_ref
  20.0 0.0 copy-start
  20.0 1.6 copy-done
  21.6 2.8 %gather_tiles.1 = bf16[16,4096]{1,0:T(8,128)(2,1)S(1)} custom-call(s32[64]{0:T(128)S(1)} %reshape_squeeze.3.src_ref, s32[64]{0:T(128)S(1)} %broadcast_select_fusion.dst_ref, bf16[16,5120]{1,0:T(8,128)(2,1)S(1)} %pad_maximum_fusion.1.x_ref, bf16[8,8,128,128]{3,2,1,0:T(8,128)(2,1)S(1)} %bitcast.49), custom_call_target="tpu_custom_call" | custom-call | tf_op jit(solution)/shard_map/gather_tiles/pallas_call | solution.py:111
  24.4 0.0 copy-done.3
  24.5 0.0 copy-start.4
  24.5 2.7 %copy.27 = bf16[2,16,4096]{1,0,2:T(2,128)(2,1)S(1)} copy(bf16[2,16,4096]{2,1,0:T(8,128)(2,1)S(1)} %pad_maximum_fusion) | data formatting | bytes 524288 | tf_op jit(solution)/shard_map/stack | solution.py:120
  27.2 0.0 copy-start.5
  27.2 2.8 %reshape.38 = bf16[8,2,8192]{2,1,0:T(2,128)(2,1)} reshape(bf16[4096,2,16]{2,1,0:T(2,128)(2,1)S(1)} %bitcast.57) | data formatting | bytes 524288
  30.1 6.2 %all-to-all-start = ((bf16[8,2,8192]{2,1,0:T(2,128)(2,1)}), bf16[8,2,8192]{2,1,0:T(2,128)(2,1)S(1)}, u32[]{:S(2)}, u32[]{:S(2)}) async-start(bf16[8,2,8192]{2,1,0:T(2,128)(2,1)} %reshape.38), calls=%async_computation | async-start | bytes 524288 | tf_op jit(solution)/shard_map/all_to_all | solution.py:119
  36.3 0.0 copy-done.4
  36.3 0.0 copy-start.6
  36.4 0.0 copy-start.7
  36.4 9.3 %all-to-all-done = bf16[8,2,8192]{2,1,0:T(2,128)(2,1)S(1)} async-done(((bf16[8,2,8192]{2,1,0:T(2,128)(2,1)}), bf16[8,2,8192]{2,1,0:T(2,128)(2,1)S(1)}, u32[]{:S(2)}, u32[]{:S(2)}) %all-to-all-start) | async-done | bytes 262176 | tf_op jit(solution)/shard_map/all_to_all | solution.py:119
  45.7 1.4 reshape.39
  47.1 1.3 copy.38
  48.4 1.1 convert_reduce_fusion
  49.6 0.3 convolution_convert_fusion
  49.8 1.0 copy.30
  50.8 3.6 %all-to-all-start.1 = ((bf16[2,128,512]{2,0,1:T(2,128)(2,1)}), bf16[2,128,512]{2,0,1:T(2,128)(2,1)S(1)}, u32[]{:S(2)}, u32[]{:S(2)}) async-start(bf16[2,128,512]{2,0,1:T(2,128)(2,1)} %copy.30), calls=%async_computation.1 | async-start | bytes 524288 | tf_op jit(solution)/shard_map/all_to_all | solution.py:135
  54.4 0.0 all-reduce.2.cloned.1.call-start
  54.4 0.9 fusion.2
  55.4 0.0 all-reduce.2.cloned.1.call-update
  55.4 40.8 %psum.15 = f32[256]{0:T(256)} all-reduce(f32[256]{0:T(256)S(1)} %get-tuple-element.9), channel_id=1, replica_groups=mesh['grp'=4,'feat'=8] {'grp','feat'}, use_global_device_ids=true, to_apply=%region_2.3 | all-reduce | flops 256 | bytes 2048 | tf_op jit(solution)/shard_map/psum | solution.py:140
  96.2 0.0 all-to-all-done.1
  96.3 0.0 copy-done.1
  96.3 0.0 copy-start.2
  96.3 2.1 %scatter_tiles.1 = (f32[16,4096]{1,0:T(8,128)S(1)}, bf16[16,1024]{1,0:T(8,128)(2,1)S(1)}) custom-call(s32[64]{0:T(128)S(1)} %reshape_squeeze.3.src_ref, s32[64]{0:T(128)S(1)} %broadcast_select_fusion.dst_ref, bf16[16,4096]{1,0:T(8,128)(2,1)S(1)} %bitcast.51, bf16[8,8,128,128]{3,2,1,0:T(8,128)(2,1)S(1)} %bitcast.50, bf16[16,4096]{1,0:T(8,128)(2,1)S(1)} %bitcast.52), custom_call_target="tpu_custom_call" | custom-call | tf_op jit(solution)/shard_map/scatter_tiles/pallas_call | solution.py:144
  98.4 0.4 copy.34
  98.8 0.5 broadcast.11
  99.3 2.3 %reduce = bf16[1024,16]{1,0:T(8,128)(2,1)S(1)} reduce(bf16[1024,1,16]{2,1,0:T(2,128)(2,1)S(1)} %bitcast.59, bf16[]{:T(256)} %broadcast.11), dimensions={1}, to_apply=%bitcast.39.reduce_sub_computation | reduce | bytes 65538
  101.6 0.9 reshape.40
  102.5 3.8 %all-to-all-start.2 = ((bf16[4,2,2048]{2,1,0:T(2,128)(2,1)}), bf16[4,2,2048]{2,1,0:T(2,128)(2,1)S(1)}, u32[]{:S(2)}, u32[]{:S(2)}) async-start(bf16[4,2,2048]{2,1,0:T(2,128)(2,1)} %reshape.40), calls=%async_computation.2 | async-start | bytes 65536 | tf_op jit(solution)/shard_map/all_to_all | solution.py:156
  106.3 80.9 %all-reduce.2.cloned.1.call-done = f32[2,128,256]{2,1,0:T(8,128)} async-done(((f32[2,128,256]{2,1,0:T(8,128)}), f32[2,128,256]{2,1,0:T(8,128)}) %all-reduce.2.cloned.1.call-update) | async-done | bytes 262160 | tf_op jit(solution)/shard_map/psum | solution.py:140
  187.2 1.3 dynamic-slice_bitcast_fusion
  188.6 0.0 all-to-all-done.2
  188.6 0.5 reshape.41
  189.0 0.3 copy.35
  189.3 0.0 copy-done.2
  189.3 1.3 add_hubs.1
  (14 shorter events, 0.1 us)
Async XLA Ops:
  7.2 17.3 %copy-start.3 = (bf16[16,4096]{1,0:T(8,128)(2,1)S(1)}, bf16[16,4096]{1,0:T(8,128)(2,1)}, u32[]{:S(2)}) copy-start(bf16[16,4096]{1,0:T(8,128)(2,1)} %param.10) | copy-start | bytes 393220
  20.0 1.6 copy-start
  24.5 11.8 %copy-start.4 = (bf16[128,256]{1,0:T(8,128)(2,1)S(1)}, bf16[128,256]{1,0:T(8,128)(2,1)}, u32[]{:S(2)}) copy-start(bf16[128,256]{1,0:T(8,128)(2,1)} %param.11) | copy-start | bytes 196612
  27.2 9.1 %copy-start.5 = (bf16[128,256]{1,0:T(8,128)(2,1)S(1)}, bf16[128,256]{1,0:T(8,128)(2,1)}, u32[]{:S(2)}) copy-start(bf16[128,256]{1,0:T(8,128)(2,1)} %param.12) | copy-start | bytes 196612
  30.1 15.6 %all-to-all-start = ((bf16[8,2,8192]{2,1,0:T(2,128)(2,1)}), bf16[8,2,8192]{2,1,0:T(2,128)(2,1)S(1)}, u32[]{:S(2)}, u32[]{:S(2)}) async-start(bf16[8,2,8192]{2,1,0:T(2,128)(2,1)} %reshape.38), calls=%async_computation | async-start | bytes 524288 | tf_op jit(solution)/shard_map/all_to_all | solution.py:119
  36.3 12.1 %copy-start.6 = (bf16[512,256]{1,0:T(8,128)(2,1)S(1)}, bf16[512,256]{1,0:T(8,128)(2,1)}, u32[]{:S(2)}) copy-start(bf16[512,256]{1,0:T(8,128)(2,1)} %param.19) | copy-start | bytes 786436
  36.4 12.1 %copy-start.7 = (f32[256]{0:T(256)S(1)}, f32[256]{0:T(256)}, u32[]{:S(2)}) copy-start(f32[256]{0:T(256)} %param.13) | copy-start | bytes 3076
  49.6 46.8 %copy-start.1 = (bf16[1,8,8,128,128]{4,3,2,1,0:T(8,128)(2,1)S(1)}, bf16[1,8,8,128,128]{4,3,2,1,0:T(8,128)(2,1)}, u32[]{:S(2)}) copy-start(bf16[1,8,8,128,128]{4,3,2,1,0:T(8,128)(2,1)} %param.14) | copy-start | bytes 6291460
  50.8 45.4 %all-to-all-start.1 = ((bf16[2,128,512]{2,0,1:T(2,128)(2,1)}), bf16[2,128,512]{2,0,1:T(2,128)(2,1)S(1)}, u32[]{:S(2)}, u32[]{:S(2)}) async-start(bf16[2,128,512]{2,0,1:T(2,128)(2,1)} %copy.30), calls=%async_computation.1 | async-start | bytes 524288 | tf_op jit(solution)/shard_map/all_to_all | solution.py:135
  54.4 132.8 %all-reduce.2.cloned.1.call-start = ((), (), s32[]{:S(2)}) async-start(), calls=%async_computation.3 | async-start | bytes 524288 | tf_op jit(solution)/shard_map/psum | solution.py:140
  96.3 93.0 %copy-start.2 = (s32[1,2]{1,0:T(1,128)S(1)}, s32[1,2]{1,0:T(1,128)}, u32[]{:S(2)}) copy-start(s32[1,2]{1,0:T(1,128)} %param.18) | copy-start | bytes 28
  102.5 86.1 %all-to-all-start.2 = ((bf16[4,2,2048]{2,1,0:T(2,128)(2,1)}), bf16[4,2,2048]{2,1,0:T(2,128)(2,1)S(1)}, u32[]{:S(2)}, u32[]{:S(2)}) async-start(bf16[4,2,2048]{2,1,0:T(2,128)(2,1)} %reshape.40), calls=%async_computation.2 | async-start | bytes 65536 | tf_op jit(solution)/shard_map/all_to_all | solution.py:156
Sparse Core Ops, SparseCore 0:
  60.7 126.4 all-reduce.1

commit v2 on v1

--- a/solution.py
+++ b/solution.py
@@ -15,6 +15,7 @@
 def gather_tiles(own_blocks, src_ref, dst_ref, x_ref, tiles_ref, out_ref):
     owners, slots, size, _ = tiles_ref.shape
     rows = x_ref.shape[0]
+    out_ref[:rows, :] = x_ref[:, : out_ref.shape[1]]
 
     def owner(o, carry):
         total = jnp.zeros((own_blocks * rows, size), jnp.float32)
@@ -28,7 +29,7 @@
                 left, tiles_ref[o, t], (((1,), (1,)), ((), ())), preferred_element_type=jnp.float32
             )
         for d in range(own_blocks):
-            out_ref[:, lanes(o * own_blocks + d, size)] = total[d * rows : (d + 1) * rows].astype(
+            out_ref[rows:, lanes(o * own_blocks + d, size)] = total[d * rows : (d + 1) * rows].astype(
                 out_ref.dtype
             )
         return carry
@@ -36,17 +37,17 @@
     lax.fori_loop(0, owners, owner, 0)
 
 
-def scatter_tiles(own_blocks, src_ref, dst_ref, g_ref, tiles_ref, self_ref, out_ref, hub_ref, total):
+def scatter_tiles(own_blocks, src_ref, dst_ref, g_ref, tiles_ref, out_ref, hub_ref, total):
     owners, slots, size, _ = tiles_ref.shape
-    nodes = g_ref.shape[1]
-    total[:, :nodes] = self_ref[...].astype(jnp.float32)
+    rows, nodes = out_ref.shape
+    total[:, :nodes] = g_ref[:rows, :].astype(jnp.float32)
     total[:, nodes:] = jnp.zeros((total.shape[0], total.shape[1] - nodes), jnp.float32)
 
     def owner(o, carry):
         terms = []
         for t in range(slots):
             dst = dst_ref[o * slots + t]
-            g = g_ref[:, lanes(o * own_blocks + jnp.maximum(dst, 0), size)]
+            g = g_ref[rows:, lanes(o * own_blocks + jnp.maximum(dst, 0), size)]
             term = jnp.dot(g, tiles_ref[o, t], preferred_element_type=jnp.float32)
             terms.append(term * (dst >= 0).astype(jnp.float32))
         for t in range(slots):
@@ -70,6 +71,85 @@
     for k in range(hubs):
         at = lanes(ids_ref[k], size)
         out_ref[:, at] = out_ref[:, at] + back[:, k * size : (k + 1) * size]
+
+
+def exchange_body(axis, cuts, joins, *refs):
+    items = len(cuts)
+    inputs, outputs, held = refs[:items], refs[items : 2 * items], refs[2 * items : 3 * items]
+    send_sem, recv_sem = refs[3 * items :]
+    peers = lax.axis_size(axis)
+    me = lax.axis_index(axis)
+
+    def block(i, peer):
+        if cuts[i] == "whole":
+            return inputs[i]
+        if cuts[i] == "lead":
+            return inputs[i].at[peer]
+        return inputs[i].at[:, lanes(peer, held[i].shape[2])]
+
+    others = [lax.rem(me + step, peers) for step in range(1, peers)]
+    barrier = pltpu.get_barrier_semaphore()
+    for peer in others:
+        pl.semaphore_signal(
+            barrier, inc=1, device_id={axis: peer}, device_id_type=pl.DeviceIdType.MESH
+        )
+    pl.semaphore_wait(barrier, peers - 1)
+    copies = []
+    for step, peer in enumerate(others):
+        for i in range(items):
+            copy = pltpu.make_async_remote_copy(
+                src_ref=block(i, peer),
+                dst_ref=held[i].at[me],
+                send_sem=send_sem.at[i, step],
+                recv_sem=recv_sem.at[i, step],
+                device_id={axis: peer},
+                device_id_type=pl.DeviceIdType.MESH,
+            )
+            copy.start()
+            copies.append(copy)
+    for i in range(items):
+        held[i][me] = block(i, me)[...]
+    for copy in copies:
+        copy.wait()
+    for i in range(items):
+        if joins[i] == "sum":
+            total = held[i][0]
+            for p in range(1, peers):
+                total += held[i][p]
+            outputs[i][...] = total
+        elif joins[i] == "lanes":
+            width = held[i].shape[2]
+            for p in range(peers):
+                outputs[i][:, p * width : (p + 1) * width] = held[i][p]
+        else:
+            outputs[i][...] = held[i][...]
+
+
+def exchange(axis, number, arrays, cuts, joins):
+    peers = lax.axis_size(axis)
+    blocks, outs = [], []
+    for array, cut, join in zip(arrays, cuts, joins):
+        if cut == "lead":
+            rows, width = array.shape[1:]
+        else:
+            rows, width = array.shape
+            width = width // peers if cut == "lanes" else width
+        blocks.append(pltpu.VMEM((peers, rows, width), array.dtype))
+        shape = {"sum": (rows, width), "lanes": (rows, peers * width)}.get(join, (peers, rows, width))
+        outs.append(jax.ShapeDtypeStruct(shape, array.dtype))
+    vmem = pl.BlockSpec(memory_space=pltpu.VMEM)
+    semaphores = pltpu.SemaphoreType.DMA((len(arrays), peers - 1))
+    return pl.pallas_call(
+        functools.partial(exchange_body, axis, cuts, joins),
+        out_shape=outs,
+        in_specs=[vmem] * len(arrays),
+        out_specs=[vmem] * len(arrays),
+        scratch_shapes=[*blocks, semaphores, semaphores],
+        compiler_params=pltpu.CompilerParams(
+            collective_id=number, has_side_effects=True, vmem_limit_bytes=40 * 1024 * 1024
+        ),
+        name=f"exchange_{number}",
+    )(*arrays)
 
 
 def local(
@@ -86,41 +166,44 @@
 ):
     columns, nodes = features.shape
     owners = lax.axis_size("feat")
-    position = lax.axis_index("feat")
     size = tile_vals.shape[-1]
     slots = tile_src.shape[2]
     own_blocks = nodes // size // owners
     hubs = hub_blocks.shape[1]
+    hidden = w_self.shape[1]
     rows = max(columns, 16)
     vmem, smem = pl.BlockSpec(memory_space=pltpu.VMEM), pl.BlockSpec(memory_space=pltpu.SMEM)
     params = pltpu.CompilerParams(vmem_limit_bytes=40 * 1024 * 1024)
 
     def padded(a):
-        return a if rows == columns else jnp.pad(a, ((0, rows - columns), (0, 0)))
-
+        spare = [(0, 0)] * a.ndim
+        spare[-2] = (0, rows - columns)
+        return a if rows == columns else jnp.pad(a, spare)
+
+    mine = padded(features)
     own_hubs = jnp.concatenate(
-        [lax.dynamic_slice_in_dim(features, hub_blocks[0, k] * size, size, 1) for k in range(hubs)],
+        [lax.dynamic_slice_in_dim(mine, hub_blocks[0, k] * size, size, 1) for k in range(hubs)],
         axis=1,
     )
-    all_hubs = lax.all_gather(own_hubs, "grp", axis=1, tiled=True)
-    combined = padded(jnp.concatenate([features, all_hubs], axis=1))
+    (all_hubs,) = exchange("grp", 0, [own_hubs], ["whole"], ["lanes"])
+    combined = jnp.concatenate([mine, all_hubs], axis=1)
     live = jnp.arange(slots, dtype=jnp.int32)[None, :] < tile_count[0][:, None]
     src = tile_src[0].reshape(-1)
     dst = jnp.where(live, tile_dst[0], -1).reshape(-1)
     tiles = tile_vals[0]
-    agg = pl.pallas_call(
+    both = pl.pallas_call(
         functools.partial(gather_tiles, own_blocks),
-        out_shape=jax.ShapeDtypeStruct((rows, nodes), jnp.bfloat16),
+        out_shape=jax.ShapeDtypeStruct((2 * rows, nodes), jnp.bfloat16),
         in_specs=[smem, smem, vmem, vmem],
         out_specs=vmem,
         compiler_params=params,
         name="gather_tiles",
-    )(src, dst, combined, tiles)[:columns]
-    both = lax.all_to_all(
-        jnp.stack([features, agg]), "feat", split_axis=2, concat_axis=1, tiled=True
-    )
-    both = both.reshape(-1, both.shape[2])
-    weights = jnp.concatenate([w_self, w_neigh], axis=0)
+    )(src, dst, combined, tiles)
+    (both,) = exchange("feat", 1, [both], ["lanes"], ["lead"])
+    both = both.reshape(owners * 2 * rows, nodes // owners)
+    weights = jnp.stack(
+        [padded(w.reshape(owners, columns, hidden)) for w in (w_self, w_neigh)], axis=1
+    ).reshape(owners * 2 * rows, hidden)
     preact = (
         lax.dot_general(both, weights, (((0,), (0,)), ((), ())), preferred_element_type=jnp.float32)
         + bias
@@ -132,14 +215,21 @@
     grads = lax.dot_general(
         weights, grad_pre, (((1,), (1,)), ((), ())), preferred_element_type=jnp.float32
     ).astype(jnp.bfloat16)
-    back = lax.all_to_all(
-        grads.reshape(2, -1, grads.shape[1]), "feat", split_axis=1, concat_axis=2, tiled=True
-    )
     weight_part = jnp.dot(both, grad_pre, preferred_element_type=jnp.float32)
     bias_part = jnp.sum(grad_pre.astype(jnp.float32), axis=0)
-    weight_sum, bias_grad = lax.psum((weight_part, bias_part), ("grp", "feat"))
-    weight_sum = lax.dynamic_slice_in_dim(
-        weight_sum.reshape(2, -1, weight_sum.shape[1]), position * columns, columns, 1
+    sums = jnp.concatenate(
+        [
+            weight_part.reshape(owners, 2 * rows, hidden),
+            jnp.broadcast_to(bias_part, (owners, 8, hidden)),
+        ],
+        axis=1,
+    )
+    back, sums = exchange(
+        "feat",
+        2,
+        [grads.reshape(owners, 2 * rows, nodes // owners), sums],
+        ["lead", "lead"],
+        ["lanes", "sum"],
     )
     part, hub_part = pl.pallas_call(
         functools.partial(scatter_tiles, own_blocks),
@@ -147,15 +237,13 @@
             jax.ShapeDtypeStruct((rows, nodes), jnp.float32),
             jax.ShapeDtypeStruct((rows, combined.shape[1] - nodes), jnp.bfloat16),
         ),
-        in_specs=[smem, smem, vmem, vmem, vmem],
+        in_specs=[smem, smem, vmem, vmem],
         out_specs=(vmem, vmem),
         scratch_shapes=[pltpu.VMEM((rows, combined.shape[1]), jnp.float32)],
         compiler_params=params,
         name="scatter_tiles",
-    )(src, dst, padded(back[1]), tiles, padded(back[0]))
-    hub_back = lax.all_to_all(
-        hub_part[None, :columns], "grp", split_axis=2, concat_axis=0, tiled=True
-    )
+    )(src, dst, back, tiles)
+    hub_back, sums = exchange("grp", 3, [hub_part, sums], ["lanes", "whole"], ["lead", "sum"])
     feat_grad = pl.pallas_call(
         add_hubs,
         out_shape=jax.ShapeDtypeStruct((columns, nodes), jnp.float32),
@@ -163,8 +251,14 @@
         out_specs=vmem,
         compiler_params=params,
         name="add_hubs",
-    )(hub_blocks[0], part[:columns], hub_back)
-    return (output, feat_grad, weight_sum[0], weight_sum[1], bias_grad)
+    )(hub_blocks[0], part[:columns], hub_back[:, :columns])
+    return (
+        output,
+        feat_grad,
+        sums[:columns],
+        sums[rows : rows + columns],
+        sums[2 * rows],
+    )
 
 
 def solution(mesh):

time: 198 us -> 54.5 us (0.28)
  the two profiles are of different devices: /device:TPU:0 before, /device:TPU:11 now
where the time goes in v2:
time: 54.5 us; the launch traced here: 54.2 us
  Pallas kernels  42.3 us (78%)
  local copies, waits for them, and re-layouts  6.49 us (12%)
  between operations  2.13 us (4%)
  other arithmetic  1.7 us (3%)
  matrix products  1.63 us (3%)
    pallas_call x4, Pallas kernels, exchange(): pl.pallas_call(functools.partial(exchange_body, axis, cuts, joins), out_s...  36.1 us
    pallas_call x1, Pallas kernels, local(): pl.pallas_call(functools.partial(gather_tiles, own_blocks), out_shape=jax...  2.82 us
    pallas_call x1, Pallas kernels, local(): pl.pallas_call(functools.partial(scatter_tiles, own_blocks), out_shape=(j...  2.1 us
    unnamed x14, local copies, waits for them, and re-layouts  1.61 us
    slice x1, local copies, waits for them, and re-layouts, local(): hub_blocks[0, k] * size  1.32 us
    pallas_call x1, Pallas kernels, local(): pl.pallas_call(add_hubs, out_shape=jax.ShapeDtypeStruct((columns, nodes),...  1.27 us
    dot_general x1, matrix products, local(): lax.dot_general(both, weights, (((0,), (0,)), ((), ())), preferred_elemen...  1.14 us

profile of v2, /device:TPU:11, one launch (start us, length us, event | category | flops | bytes accessed | tf_op | source)
XLA Modules:
  0.0 54.2 jit_solution(8238909706462741003)
XLA Ops:
  0.6 0.0 copy-start.5
  0.6 0.0 copy-start.6
  0.7 0.0 copy-start.3
  0.7 0.0 copy-start.4
  0.7 0.8 %reshape_squeeze.3.src_ref = s32[64]{0:T(128)S(1)} reshape(s32[1,8,8]{2,1,0:T(8,128)} %param.15) | data formatting | bytes 512 | tf_op jit(solution)/shard_map/reshape;squeeze | solution.py:191
  1.5 0.8 %squeeze.14 = s32[64]{0:T(128)S(1)} reshape(s32[1,8,8]{2,1,0:T(8,128)} %param.16) | data formatting | bytes 512 | tf_op jit(solution)/shard_map/squeeze | solution.py:192
  2.3 0.7 %iota_compare_fusion = pred[8,8]{1,0:T(8,128)(4,1)S(1)} fusion(s32[8]{0:T(128)} %bitcast.29), kind=kLoop, calls=%fused_computation.12 | loop fusion | flops 64 | bytes 96 | tf_op jit(solution)/shard_map/lt | solution.py:190
  3.0 0.1 lt.29
  3.1 1.3 %fusion.3 = (s32[1,1]{1,0:T(1,128)}, s32[1,1]{1,0:T(1,128)}) fusion(s32[1,2]{1,0:T(1,128)} %param.18), kind=kLoop, calls=%fused_computation.17 | loop fusion | bytes 16 | tf_op jit(solution)/shard_map/slice | solution.py:185
  5.7 0.7 %constant_dynamic-slice_fusion.1 = (bf16[16,128]{1,0:T(8,128)(2,1)S(1)}, bf16[16,128]{1,0:T(8,128)(2,1)S(1)}) fusion(bf16[16,4096]{1,0:T(8,128)(2,1)} %param.10, s32[]{:T(128)S(6)} %select_n.12, s32[]{:T(128)S(6)} %select_n.13), kind=kLoop, calls=%fused_computation.14 | loop fusion | bytes 16392 | tf_op jit(solution)/shard_map/dynamic_slice | solution.py:185
  6.4 4.0 %exchange_0.1 = bf16[16,1024]{1,0:T(8,128)(2,1)S(1)} custom-call(bf16[16,256]{1,0:T(8,128)(2,1)S(1)} %pad_maximum_fusion.3.refs_0_), custom_call_target="tpu_custom_call" | custom-call | tf_op jit(solution)/shard_map/exchange_0/pallas_call | solution.py:142
  10.4 0.9 %pad_maximum_fusion.1.x_ref = bf16[16,5120]{1,0:T(8,128)(2,1)S(1)} fusion(bf16[16,1024]{1,0:T(8,128)(2,1)S(1)} %exchange_0.1, bf16[16,4096]{1,0:T(8,128)(2,1)} %param.10), kind=kLoop, calls=%fused_computation.9 | loop fusion | flops 327680 | bytes 327680 | tf_op jit(solution)/shard_map/concatenate | solution.py:189
  11.3 0.0 copy-start
  11.3 1.6 %copy-done = bf16[1,8,8,128,128]{4,3,2,1,0:T(8,128)(2,1)S(1)} copy-done((bf16[1,8,8,128,128]{4,3,2,1,0:T(8,128)(2,1)S(1)}, bf16[1,8,8,128,128]{4,3,2,1,0:T(8,128)(2,1)}, u32[]{:S(2)}) %copy-start) | copy-done | bytes 2097176
  12.9 2.8 %gather_tiles.1.refs_0_ = bf16[32,4096]{1,0:T(8,128)(2,1)S(1)} custom-call(s32[64]{0:T(128)S(1)} %reshape_squeeze.3.src_ref, s32[64]{0:T(128)S(1)} %broadcast_select_fusion.dst_ref, bf16[16,5120]{1,0:T(8,128)(2,1)S(1)} %pad_maximum_fusion.1.x_ref, bf16[8,8,128,128]{3,2,1,0:T(8,128)(2,1)S(1)} %bitcast.19), custom_call_target="tpu_custom_call" | custom-call | tf_op jit(solution)/shard_map/gather_tiles/pallas_call | solution.py:194
  15.8 10.5 %exchange_1.1 = bf16[8,32,512]{2,1,0:T(8,128)(2,1)S(1)} custom-call(bf16[32,4096]{1,0:T(8,128)(2,1)S(1)} %gather_tiles.1.refs_0_), custom_call_target="tpu_custom_call" | custom-call | tf_op jit(solution)/shard_map/exchange_1/pallas_call | solution.py:142
  26.2 0.0 copy-done.3
  26.2 0.0 copy-done.4
  26.3 0.0 copy-done.5
  26.3 0.0 copy-done.6
  26.3 1.1 %convert_reduce_fusion = (f32[256]{0:T(256)S(1)}, bf16[512,256]{1,0:T(8,128)(2,1)S(1)}, bf16[512,256]{1,0:T(8,128)(2,1)}) fusion(bf16[512,256]{1,0:T(8,128)(2,1)S(1)} %copy-done.5, f32[256]{0:T(256)S(1)} %copy-done.6, bf16[256,512]{1,0:T(8,128)(2,1)S(1)} %bitcast.21, bf16[256,256]{1,0:T(8,128)(2,1)S(1)} %bitcast.24), kind=kOutput, calls=%fused_computation.2 | convolution fusion | flops 69074688 | bytes 1181696 | tf_op jit(solution)/shard_map/dot_general | solution.py:208
  27.4 0.0 copy-start.1
  27.4 0.2 fusion
  27.7 0.0 copy-start.2
  27.7 0.3 convolution_convert_fusion
  28.0 15.3 %exchange_2.1 = (bf16[32,4096]{1,0:T(8,128)(2,1)S(1)}, f32[40,256]{1,0:T(8,128)S(1)}) custom-call(bf16[8,32,512]{2,1,0:T(8,128)(2,1)S(1)} %bitcast.22, f32[8,40,256]{2,1,0:T(8,128)S(1)} %pad_maximum_fusion.refs_1_), custom_call_target="tpu_custom_call" | custom-call | tf_op jit(solution)/shard_map/exchange_2/pallas_call | solution.py:142
  43.3 0.0 copy-done.1
  43.3 2.1 %scatter_tiles.1 = (f32[16,4096]{1,0:T(8,128)S(1)}, bf16[16,1024]{1,0:T(8,128)(2,1)S(1)}) custom-call(s32[64]{0:T(128)S(1)} %reshape_squeeze.3.src_ref, s32[64]{0:T(128)S(1)} %broadcast_select_fusion.dst_ref, bf16[32,4096]{1,0:T(8,128)(2,1)S(1)} %get-tuple-element.11.g_ref, bf16[8,8,128,128]{3,2,1,0:T(8,128)(2,1)S(1)} %bitcast.20), custom_call_target="tpu_custom_call" | custom-call | tf_op jit(solution)/shard_map/scatter_tiles/pallas_call | solution.py:234
  45.4 6.4 %exchange_3.1 = (bf16[4,16,256]{2,1,0:T(8,128)(2,1)S(1)}, f32[40,256]{1,0:T(8,128)S(1)}) custom-call(bf16[16,1024]{1,0:T(8,128)(2,1)S(1)} %get-tuple-element.13.refs_0_, f32[40,256]{1,0:T(8,128)S(1)} %get-tuple-element.14.refs_1_), custom_call_target="tpu_custom_call" | custom-call | tf_op jit(solution)/shard_map/exchange_3/pallas_call | solution.py:142
  51.8 0.0 copy-done.2
  51.8 1.3 %add_hubs.1 = f32[16,4096]{1,0:T(8,128)} custom-call(s32[2]{0:T(128)S(1)} %bitcast.23, f32[16,4096]{1,0:T(8,128)S(1)} %get-tuple-element.12.part_ref, bf16[4,16,256]{2,1,0:T(8,128)(2,1)S(1)} %get-tuple-element.15.hub_ref), custom_call_target="tpu_custom_call" | custom-call | tf_op jit(solution)/shard_map/add_hubs/pallas_call | solution.py:247
  53.0 0.6 %slice.19 = f32[1,256]{1,0:T(1,128)} slice(f32[40,256]{1,0:T(8,128)S(1)} %get-tuple-element.16), slice={[32:33], [0:256]} | slice | bytes 2048 | tf_op jit(solution)/shard_map/slice | solution.py:260
  53.6 0.6 %fusion.2 = (f32[16,256]{1,0:T(8,128)}, f32[16,256]{1,0:T(8,128)}) fusion(f32[40,256]{1,0:T(8,128)S(1)} %get-tuple-element.16), kind=kLoop, calls=%fused_computation.16 | loop fusion | bytes 65536 | tf_op jit(solution)/shard_map/slice | solution.py:259
  (5 shorter events, 0.1 us)
Async XLA Ops:
  0.6 25.6 %copy-start.5 = (bf16[512,256]{1,0:T(8,128)(2,1)S(1)}, bf16[512,256]{1,0:T(8,128)(2,1)}, u32[]{:S(2)}) copy-start(bf16[512,256]{1,0:T(8,128)(2,1)} %param.19) | copy-start | bytes 786436
  0.6 25.6 %copy-start.6 = (f32[256]{0:T(256)S(1)}, f32[256]{0:T(256)}, u32[]{:S(2)}) copy-start(f32[256]{0:T(256)} %param.13) | copy-start | bytes 3076
  0.7 25.6 %copy-start.3 = (bf16[128,256]{1,0:T(8,128)(2,1)S(1)}, bf16[128,256]{1,0:T(8,128)(2,1)}, u32[]{:S(2)}) copy-start(bf16[128,256]{1,0:T(8,128)(2,1)} %param.12) | copy-start | bytes 196612
  0.7 25.6 %copy-start.4 = (bf16[128,256]{1,0:T(8,128)(2,1)S(1)}, bf16[128,256]{1,0:T(8,128)(2,1)}, u32[]{:S(2)}) copy-start(bf16[128,256]{1,0:T(8,128)(2,1)} %param.11) | copy-start | bytes 196612
  11.3 1.6 %copy-start = (bf16[1,8,8,128,128]{4,3,2,1,0:T(8,128)(2,1)S(1)}, bf16[1,8,8,128,128]{4,3,2,1,0:T(8,128)(2,1)}, u32[]{:S(2)}) copy-start(bf16[1,8,8,128,128]{4,3,2,1,0:T(8,128)(2,1)} %param.14) | copy-start | bytes 6291460
  27.4 15.8 %copy-start.1 = (bf16[1,8,8,128,128]{4,3,2,1,0:T(8,128)(2,1)S(1)}, bf16[1,8,8,128,128]{4,3,2,1,0:T(8,128)(2,1)}, u32[]{:S(2)}) copy-start(bf16[1,8,8,128,128]{4,3,2,1,0:T(8,128)(2,1)} %param.14) | copy-start | bytes 6291460
  27.7 24.1 %copy-start.2 = (s32[1,2]{1,0:T(1,128)S(1)}, s32[1,2]{1,0:T(1,128)}, u32[]{:S(2)}) copy-start(s32[1,2]{1,0:T(1,128)} %param.18) | copy-start | bytes 28

commit v3 on v2

--- a/solution.py
+++ b/solution.py
@@ -12,21 +12,30 @@
     return pl.ds(pl.multiple_of(index * width, width), width)
 
 
-def gather_tiles(own_blocks, src_ref, dst_ref, x_ref, tiles_ref, out_ref):
-    owners, slots, size, _ = tiles_ref.shape
+def destination(dst_ref, count_ref, o, t):
+    return jnp.where(t < count_ref[0, o], dst_ref[0, o, t], -1)
+
+
+def gather_tiles(
+    own_blocks, src_ref, dst_ref, count_ref, features_ref, hubs_ref, tiles_ref, out_ref, x_ref
+):
+    _, owners, slots, size, _ = tiles_ref.shape
     rows = x_ref.shape[0]
-    out_ref[:rows, :] = x_ref[:, : out_ref.shape[1]]
+    nodes = out_ref.shape[1]
+    out_ref[:rows, :] = features_ref[...]
+    x_ref[:, :nodes] = features_ref[...]
+    x_ref[:, nodes:] = hubs_ref[...]
 
     def owner(o, carry):
         total = jnp.zeros((own_blocks * rows, size), jnp.float32)
         for t in range(slots):
-            x = x_ref[:, lanes(src_ref[o * slots + t], size)].astype(jnp.float32)
-            dst = dst_ref[o * slots + t]
+            x = x_ref[:, lanes(src_ref[0, o, t], size)].astype(jnp.float32)
+            dst = destination(dst_ref, count_ref, o, t)
             left = jnp.concatenate(
                 [x * (dst == d).astype(jnp.float32) for d in range(own_blocks)], axis=0
             ).astype(jnp.bfloat16)
             total += lax.dot_general(
-                left, tiles_ref[o, t], (((1,), (1,)), ((), ())), preferred_element_type=jnp.float32
+                left, tiles_ref[0, o, t], (((1,), (1,)), ((), ())), preferred_element_type=jnp.float32
             )
         for d in range(own_blocks):
             out_ref[rows:, lanes(o * own_blocks + d, size)] = total[d * rows : (d + 1) * rows].astype(
@@ -37,8 +46,8 @@
     lax.fori_loop(0, owners, owner, 0)
 
 
-def scatter_tiles(own_blocks, src_ref, dst_ref, g_ref, tiles_ref, out_ref, hub_ref, total):
-    owners, slots, size, _ = tiles_ref.shape
+def scatter_tiles(own_blocks, src_ref, dst_ref, count_ref, g_ref, tiles_ref, out_ref, hub_ref, total):
+    _, owners, slots, size, _ = tiles_ref.shape
     rows, nodes = out_ref.shape
     total[:, :nodes] = g_ref[:rows, :].astype(jnp.float32)
     total[:, nodes:] = jnp.zeros((total.shape[0], total.shape[1] - nodes), jnp.float32)
@@ -46,12 +55,12 @@
     def owner(o, carry):
         terms = []
         for t in range(slots):
-            dst = dst_ref[o * slots + t]
+            dst = destination(dst_ref, count_ref, o, t)
             g = g_ref[rows:, lanes(o * own_blocks + jnp.maximum(dst, 0), size)]
-            term = jnp.dot(g, tiles_ref[o, t], preferred_element_type=jnp.float32)
+            term = jnp.dot(g, tiles_ref[0, o, t], preferred_element_type=jnp.float32)
             terms.append(term * (dst >= 0).astype(jnp.float32))
         for t in range(slots):
-            at = lanes(src_ref[o * slots + t], size)
+            at = lanes(src_ref[0, o, t], size)
             total[:, at] = total[:, at] + terms[t]
         return carry
 
@@ -60,16 +69,23 @@
     hub_ref[...] = total[:, nodes:].astype(hub_ref.dtype)
 
 
+def pick_hubs(ids_ref, features_ref, out_ref):
+    hubs = ids_ref.shape[1]
+    size = out_ref.shape[1] // hubs
+    for k in range(hubs):
+        out_ref[:, k * size : (k + 1) * size] = features_ref[:, lanes(ids_ref[0, k], size)]
+
+
 def add_hubs(ids_ref, part_ref, hub_ref, out_ref):
     peers, _, width = hub_ref.shape
-    hubs = ids_ref.shape[0]
+    hubs = ids_ref.shape[1]
     size = width // hubs
     out_ref[...] = part_ref[...]
     back = hub_ref[0].astype(jnp.float32)
     for p in range(1, peers):
         back += hub_ref[p].astype(jnp.float32)
     for k in range(hubs):
-        at = lanes(ids_ref[k], size)
+        at = lanes(ids_ref[0, k], size)
         out_ref[:, at] = out_ref[:, at] + back[:, k * size : (k + 1) * size]
 
 
@@ -95,8 +111,8 @@
         )
     pl.semaphore_wait(barrier, peers - 1)
     copies = []
-    for step, peer in enumerate(others):
-        for i in range(items):
+    for i in range(items):
+        for step, peer in enumerate(others):
             copy = pltpu.make_async_remote_copy(
                 src_ref=block(i, peer),
                 dst_ref=held[i].at[me],
@@ -113,9 +129,9 @@
         copy.wait()
     for i in range(items):
         if joins[i] == "sum":
-            total = held[i][0]
+            total = held[i][0].astype(jnp.float32)
             for p in range(1, peers):
-                total += held[i][p]
+                total += held[i][p].astype(jnp.float32)
             outputs[i][...] = total
         elif joins[i] == "lanes":
             width = held[i].shape[2]
@@ -136,7 +152,7 @@
             width = width // peers if cut == "lanes" else width
         blocks.append(pltpu.VMEM((peers, rows, width), array.dtype))
         shape = {"sum": (rows, width), "lanes": (rows, peers * width)}.get(join, (peers, rows, width))
-        outs.append(jax.ShapeDtypeStruct(shape, array.dtype))
+        outs.append(jax.ShapeDtypeStruct(shape, jnp.float32 if join == "sum" else array.dtype))
     vmem = pl.BlockSpec(memory_space=pltpu.VMEM)
     semaphores = pltpu.SemaphoreType.DMA((len(arrays), peers - 1))
     return pl.pallas_call(
@@ -167,9 +183,7 @@
     columns, nodes = features.shape
     owners = lax.axis_size("feat")
     size = tile_vals.shape[-1]
-    slots = tile_src.shape[2]
     own_blocks = nodes // size // owners
-    hubs = hub_blocks.shape[1]
     hidden = w_self.shape[1]
     rows = max(columns, 16)
     vmem, smem = pl.BlockSpec(memory_space=pltpu.VMEM), pl.BlockSpec(memory_space=pltpu.SMEM)
@@ -181,24 +195,25 @@
         return a if rows == columns else jnp.pad(a, spare)
 
     mine = padded(features)
-    own_hubs = jnp.concatenate(
-        [lax.dynamic_slice_in_dim(mine, hub_blocks[0, k] * size, size, 1) for k in range(hubs)],
-        axis=1,
-    )
+    own_hubs = pl.pallas_call(
+        pick_hubs,
+        out_shape=jax.ShapeDtypeStruct((rows, hub_blocks.shape[1] * size), mine.dtype),
+        in_specs=[smem, vmem],
+        out_specs=vmem,
+        compiler_params=params,
+        name="pick_hubs",
+    )(hub_blocks, mine)
     (all_hubs,) = exchange("grp", 0, [own_hubs], ["whole"], ["lanes"])
-    combined = jnp.concatenate([mine, all_hubs], axis=1)
-    live = jnp.arange(slots, dtype=jnp.int32)[None, :] < tile_count[0][:, None]
-    src = tile_src[0].reshape(-1)
-    dst = jnp.where(live, tile_dst[0], -1).reshape(-1)
-    tiles = tile_vals[0]
+    slot_nodes = nodes + all_hubs.shape[1]
     both = pl.pallas_call(
         functools.partial(gather_tiles, own_blocks),
         out_shape=jax.ShapeDtypeStruct((2 * rows, nodes), jnp.bfloat16),
-        in_specs=[smem, smem, vmem, vmem],
+        in_specs=[smem, smem, smem, vmem, vmem, vmem],
         out_specs=vmem,
+        scratch_shapes=[pltpu.VMEM((rows, slot_nodes), jnp.bfloat16)],
         compiler_params=params,
         name="gather_tiles",
-    )(src, dst, combined, tiles)
+    )(tile_src, tile_dst, tile_count, mine, all_hubs, tile_vals)
     (both,) = exchange("feat", 1, [both], ["lanes"], ["lead"])
     both = both.reshape(owners * 2 * rows, nodes // owners)
     weights = jnp.stack(
@@ -220,10 +235,10 @@
     sums = jnp.concatenate(
         [
             weight_part.reshape(owners, 2 * rows, hidden),
-            jnp.broadcast_to(bias_part, (owners, 8, hidden)),
+            jnp.broadcast_to(bias_part, (owners, 16, hidden)),
         ],
         axis=1,
-    )
+    ).astype(jnp.bfloat16)
     back, sums = exchange(
         "feat",
         2,
@@ -235,14 +250,14 @@
         functools.partial(scatter_tiles, own_blocks),
         out_shape=(
             jax.ShapeDtypeStruct((rows, nodes), jnp.float32),
-            jax.ShapeDtypeStruct((rows, combined.shape[1] - nodes), jnp.bfloat16),
+            jax.ShapeDtypeStruct((rows, slot_nodes - nodes), jnp.bfloat16),
         ),
-        in_specs=[smem, smem, vmem, vmem],
+        in_specs=[smem, smem, smem, vmem, vmem],
         out_specs=(vmem, vmem),
-        scratch_shapes=[pltpu.VMEM((rows, combined.shape[1]), jnp.float32)],
+        scratch_shapes=[pltpu.VMEM((rows, slot_nodes), jnp.float32)],
         compiler_params=params,
         name="scatter_tiles",
-    )(src, dst, back, tiles)
+    )(tile_src, tile_dst, tile_count, back, tile_vals)
     hub_back, sums = exchange("grp", 3, [hub_part, sums], ["lanes", "whole"], ["lead", "sum"])
     feat_grad = pl.pallas_call(
         add_hubs,
@@ -251,7 +266,7 @@
         out_specs=vmem,
         compiler_params=params,
         name="add_hubs",
-    )(hub_blocks[0], part[:columns], hub_back[:, :columns])
+    )(hub_blocks, part[:columns], hub_back[:, :columns])
     return (
         output,
         feat_grad,

time: 54.5 us -> 52.9 us (0.971)
  the two profiles are of different devices: /device:TPU:11 before, /device:TPU:0 now
where the time goes in v3:
time: 52.9 us; the launch traced here: 52.6 us
  Pallas kernels  41.8 us (79%)
  local copies, waits for them, and re-layouts  7.29 us (14%)
  matrix products  1.54 us (3%)
  other arithmetic  1.14 us (2%)
  between operations  0.83 us (2%)
    pallas_call x4, Pallas kernels, exchange(): pl.pallas_call(functools.partial(exchange_body, axis, cuts, joins), out_s...  34.8 us
    unnamed x28, local copies, waits for them, and re-layouts  6.11 us
    pallas_call x1, Pallas kernels, local(): pl.pallas_call(functools.partial(gather_tiles, own_blocks), out_shape=jax...  2.98 us
    pallas_call x1, Pallas kernels, local(): pl.pallas_call(functools.partial(scatter_tiles, own_blocks), out_shape=(j...  2.23 us
    pallas_call x1, Pallas kernels, local(): pl.pallas_call(add_hubs, out_shape=jax.ShapeDtypeStruct((columns, nodes),...  1.27 us

profile of v3, /device:TPU:0, one launch (start us, length us, event | category | flops | bytes accessed | tf_op | source)
XLA Modules:
  0.0 52.6 jit_solution(17872253396754780977)
XLA Ops:
  0.6 0.0 copy-start.13
  0.6 0.0 copy-start.2
  0.7 0.9 %copy-done.2 = bf16[16,4096]{1,0:T(8,128)(2,1)S(1)} copy-done((bf16[16,4096]{1,0:T(8,128)(2,1)S(1)}, bf16[16,4096]{1,0:T(8,128)(2,1)}, u32[]{:S(2)}) %copy-start.2) | copy-done | bytes 131096
  1.6 0.0 copy-start.8
  1.6 0.7 %copy-done.8 = s32[1,2]{1,0:T(1,128)S(1)} copy-done((s32[1,2]{1,0:T(1,128)S(1)}, s32[1,2]{1,0:T(1,128)}, u32[]{:S(2)}) %copy-start.8) | copy-done | bytes 32
  2.2 0.5 %pick_hubs.1.refs_0_ = bf16[16,256]{1,0:T(8,128)(2,1)S(1)} custom-call(s32[1,2]{1,0:T(1,128)S(1)} %copy-done.8, bf16[16,4096]{1,0:T(8,128)(2,1)S(1)} %copy-done.2), custom_call_target="tpu_custom_call" | custom-call | tf_op jit(solution)/shard_map/pick_hubs/pallas_call | solution.py:198
  2.8 4.7 %exchange_0.1.hubs_ref = bf16[16,1024]{1,0:T(8,128)(2,1)S(1)} custom-call(bf16[16,256]{1,0:T(8,128)(2,1)S(1)} %pick_hubs.1.refs_0_), custom_call_target="tpu_custom_call" | custom-call | tf_op jit(solution)/shard_map/exchange_0/pallas_call | solution.py:158
  7.5 0.9 %pad_maximum_fusion.1 = bf16[8,2,16,256]{3,2,1,0:T(8,128)(2,1)S(1)} fusion(bf16[8,1,16,256]{3,2,1,0:T(8,128)(2,1)} %bitcast.18, bf16[8,1,16,256]{3,2,1,0:T(8,128)(2,1)} %bitcast.19), kind=kLoop, calls=%fused_computation.8 | loop fusion | flops 65536 | bytes 262144 | tf_op jit(solution)/shard_map/stack | solution.py:219
  8.4 0.0 copy-start
  8.4 1.6 %copy-done = bf16[1,8,8,128,128]{4,3,2,1,0:T(8,128)(2,1)S(1)} copy-done((bf16[1,8,8,128,128]{4,3,2,1,0:T(8,128)(2,1)S(1)}, bf16[1,8,8,128,128]{4,3,2,1,0:T(8,128)(2,1)}, u32[]{:S(2)}) %copy-start) | copy-done | bytes 2097176
  10.0 0.0 copy-start.3
  10.0 0.9 %copy-done.3 = bf16[16,4096]{1,0:T(8,128)(2,1)S(1)} copy-done((bf16[16,4096]{1,0:T(8,128)(2,1)S(1)}, bf16[16,4096]{1,0:T(8,128)(2,1)}, u32[]{:S(2)}) %copy-start.3) | copy-done | bytes 131096
  10.9 0.0 copy-start.4
  10.9 0.7 %copy-done.4 = s32[1,8,8]{2,1,0:T(8,128)S(1)} copy-done((s32[1,8,8]{2,1,0:T(8,128)S(1)}, s32[1,8,8]{2,1,0:T(8,128)}, u32[]{:S(2)}) %copy-start.4) | copy-done | bytes 280
  11.6 0.0 copy-start.6
  11.6 0.7 %copy-done.6 = s32[1,8,8]{2,1,0:T(8,128)S(1)} copy-done((s32[1,8,8]{2,1,0:T(8,128)S(1)}, s32[1,8,8]{2,1,0:T(8,128)}, u32[]{:S(2)}) %copy-start.6) | copy-done | bytes 280
  12.3 0.0 copy-start.10
  12.3 0.7 %copy-done.10 = s32[1,8]{1,0:T(1,128)S(1)} copy-done((s32[1,8]{1,0:T(1,128)S(1)}, s32[1,8]{1,0:T(1,128)}, u32[]{:S(2)}) %copy-start.10) | copy-done | bytes 56
  12.9 3.0 %gather_tiles.1.refs_0_ = bf16[32,4096]{1,0:T(8,128)(2,1)S(1)} custom-call(s32[1,8,8]{2,1,0:T(8,128)S(1)} %copy-done.4, s32[1,8,8]{2,1,0:T(8,128)S(1)} %copy-done.6, s32[1,8]{1,0:T(1,128)S(1)} %copy-done.10, bf16[16,4096]{1,0:T(8,128)(2,1)S(1)} %copy-done.3, bf16[16,1024]{1,0:T(8,128)(2,1)S(1)} %exchange_0.1.hubs_ref, bf16[1,8,8,128,128]{4,3,2,1,0:T(8,128)(2,1)S(1)} %copy-done), custom_call_target="tpu_custom_call" | custom-call | tf_op jit(solution)/shard_map/gather_tiles/pallas_call | solution.py:208
  15.9 0.0 copy-start.12
  15.9 10.1 %exchange_1.1 = bf16[8,32,512]{2,1,0:T(8,128)(2,1)S(1)} custom-call(bf16[32,4096]{1,0:T(8,128)(2,1)S(1)} %gather_tiles.1.refs_0_), custom_call_target="tpu_custom_call" | custom-call | tf_op jit(solution)/shard_map/exchange_1/pallas_call | solution.py:158
  26.0 0.0 copy-done.13
  26.0 1.1 %multiply_convert_fusion.1 = (bf16[512,256]{1,0:T(8,128)(2,1)}, f32[512,256]{1,0:T(8,128)S(1)}) fusion(f32[256]{0:T(256)S(1)} %copy-done.13, bf16[256,512]{1,0:T(8,128)(2,1)S(1)} %bitcast.15, bf16[256,256]{1,0:T(8,128)(2,1)S(1)} %bitcast.16), kind=kOutput, calls=%fused_computation.4 | convolution fusion | flops 67895296 | bytes 1180672 | tf_op jit(solution)/shard_map/dot_general | solution.py:223
  27.1 0.0 copy-start.1
  27.1 0.0 copy-start.5
  27.1 0.0 copy-start.7
  27.1 0.0 copy-start.11
  27.1 0.0 copy-done.12
  27.1 0.2 fusion.1
  27.3 0.2 convolution_convert_fusion.1
  27.6 0.0 copy-start.9
  27.6 0.3 convolution_convert_fusion
  27.9 14.9 %exchange_2.1 = (bf16[32,4096]{1,0:T(8,128)(2,1)S(1)}, f32[48,256]{1,0:T(8,128)S(1)}) custom-call(bf16[8,32,512]{2,1,0:T(8,128)(2,1)S(1)} %bitcast.14, bf16[8,48,256]{2,1,0:T(8,128)(2,1)S(1)} %pad_maximum_fusion.refs_1_), custom_call_target="tpu_custom_call" | custom-call | tf_op jit(solution)/shard_map/exchange_2/pallas_call | solution.py:158
  42.8 0.0 copy-done.1
  42.8 0.0 copy-done.5
  42.8 0.0 copy-done.7
  42.8 0.0 copy-done.11
  42.8 2.2 %scatter_tiles.1 = (f32[16,4096]{1,0:T(8,128)S(1)}, bf16[16,1024]{1,0:T(8,128)(2,1)S(1)}) custom-call(s32[1,8,8]{2,1,0:T(8,128)S(1)} %copy-done.5, s32[1,8,8]{2,1,0:T(8,128)S(1)} %copy-done.7, s32[1,8]{1,0:T(1,128)S(1)} %copy-done.11, bf16[32,4096]{1,0:T(8,128)(2,1)S(1)} %get-tuple-element.11.g_ref, bf16[1,8,8,128,128]{4,3,2,1,0:T(8,128)(2,1)S(1)} %copy-done.1), custom_call_target="tpu_custom_call" | custom-call | tf_op jit(solution)/shard_map/scatter_tiles/pallas_call | solution.py:249
  45.1 5.1 %exchange_3.1 = (bf16[4,16,256]{2,1,0:T(8,128)(2,1)S(1)}, f32[48,256]{1,0:T(8,128)S(1)}) custom-call(bf16[16,1024]{1,0:T(8,128)(2,1)S(1)} %get-tuple-element.13.refs_0_, f32[48,256]{1,0:T(8,128)S(1)} %get-tuple-element.14.refs_1_), custom_call_target="tpu_custom_call" | custom-call | tf_op jit(solution)/shard_map/exchange_3/pallas_call | solution.py:158
  50.1 0.0 copy-done.9
  50.2 1.3 %add_hubs.1 = f32[16,4096]{1,0:T(8,128)} custom-call(s32[1,2]{1,0:T(1,128)S(1)} %copy-done.9, f32[16,4096]{1,0:T(8,128)S(1)} %get-tuple-element.12.part_ref, bf16[4,16,256]{2,1,0:T(8,128)(2,1)S(1)} %get-tuple-element.15.hub_ref), custom_call_target="tpu_custom_call" | custom-call | tf_op jit(solution)/shard_map/add_hubs/pallas_call | solution.py:262
  51.4 0.6 %slice.11 = f32[1,256]{1,0:T(1,128)} slice(f32[48,256]{1,0:T(8,128)S(1)} %get-tuple-element.16), slice={[32:33], [0:256]} | slice | bytes 2048 | tf_op jit(solution)/shard_map/slice | solution.py:275
  52.0 0.6 %fusion.2 = (f32[16,256]{1,0:T(8,128)}, f32[16,256]{1,0:T(8,128)}) fusion(f32[48,256]{1,0:T(8,128)S(1)} %get-tuple-element.16), kind=kLoop, calls=%fused_computation.10 | loop fusion | bytes 65536 | tf_op jit(solution)/shard_map/slice | solution.py:274
  (2 shorter events, 0.0 us)
Async XLA Ops:
  0.6 25.4 %copy-start.13 = (f32[256]{0:T(256)S(1)}, f32[256]{0:T(256)}, u32[]{:S(2)}) copy-start(f32[256]{0:T(256)} %param.13) | copy-start | bytes 3076
  0.6 0.9 %copy-start.2 = (bf16[16,4096]{1,0:T(8,128)(2,1)S(1)}, bf16[16,4096]{1,0:T(8,128)(2,1)}, u32[]{:S(2)}) copy-start(bf16[16,4096]{1,0:T(8,128)(2,1)} %features_ref.3) | copy-start | bytes 393220
  1.6 0.7 %copy-start.8 = (s32[1,2]{1,0:T(1,128)S(1)}, s32[1,2]{1,0:T(1,128)}, u32[]{:S(2)}) copy-start(s32[1,2]{1,0:T(1,128)} %ids_ref.3) | copy-start | bytes 28
  8.4 1.6 %copy-start = (bf16[1,8,8,128,128]{4,3,2,1,0:T(8,128)(2,1)S(1)}, bf16[1,8,8,128,128]{4,3,2,1,0:T(8,128)(2,1)}, u32[]{:S(2)}) copy-start(bf16[1,8,8,128,128]{4,3,2,1,0:T(8,128)(2,1)} %tiles_ref.3) | copy-start | bytes 6291460
  10.0 0.9 %copy-start.3 = (bf16[16,4096]{1,0:T(8,128)(2,1)S(1)}, bf16[16,4096]{1,0:T(8,128)(2,1)}, u32[]{:S(2)}) copy-start(bf16[16,4096]{1,0:T(8,128)(2,1)} %features_ref.3) | copy-start | bytes 393220
  10.9 0.7 %copy-start.4 = (s32[1,8,8]{2,1,0:T(8,128)S(1)}, s32[1,8,8]{2,1,0:T(8,128)}, u32[]{:S(2)}) copy-start(s32[1,8,8]{2,1,0:T(8,128)} %src_ref.3) | copy-start | bytes 772
  11.6 0.7 %copy-start.6 = (s32[1,8,8]{2,1,0:T(8,128)S(1)}, s32[1,8,8]{2,1,0:T(8,128)}, u32[]{:S(2)}) copy-start(s32[1,8,8]{2,1,0:T(8,128)} %dst_ref.3) | copy-start | bytes 772
  12.3 0.7 %copy-start.10 = (s32[1,8]{1,0:T(1,128)S(1)}, s32[1,8]{1,0:T(1,128)}, u32[]{:S(2)}) copy-start(s32[1,8]{1,0:T(1,128)} %count_ref.3) | copy-start | bytes 100
  15.9 11.2 %copy-start.12 = (bf16[512,256]{1,0:T(8,128)(2,1)S(1)}, bf16[512,256]{1,0:T(8,128)(2,1)}, u32[]{:S(2)}) copy-start(bf16[512,256]{1,0:T(8,128)(2,1)} %param.19) | copy-start | bytes 786436
  27.1 15.7 %copy-start.1 = (bf16[1,8,8,128,128]{4,3,2,1,0:T(8,128)(2,1)S(1)}, bf16[1,8,8,128,128]{4,3,2,1,0:T(8,128)(2,1)}, u32[]{:S(2)}) copy-start(bf16[1,8,8,128,128]{4,3,2,1,0:T(8,128)(2,1)} %tiles_ref.3) | copy-start | bytes 6291460
  27.1 15.7 %copy-start.5 = (s32[1,8,8]{2,1,0:T(8,128)S(1)}, s32[1,8,8]{2,1,0:T(8,128)}, u32[]{:S(2)}) copy-start(s32[1,8,8]{2,1,0:T(8,128)} %src_ref.3) | copy-start | bytes 772
  27.1 15.7 %copy-start.7 = (s32[1,8,8]{2,1,0:T(8,128)S(1)}, s32[1,8,8]{2,1,0:T(8,128)}, u32[]{:S(2)}) copy-start(s32[1,8,8]{2,1,0:T(8,128)} %dst_ref.3) | copy-start | bytes 772
  27.1 15.7 %copy-start.11 = (s32[1,8]{1,0:T(1,128)S(1)}, s32[1,8]{1,0:T(1,128)}, u32[]{:S(2)}) copy-start(s32[1,8]{1,0:T(1,128)} %count_ref.3) | copy-start | bytes 100
  27.6 22.6 %copy-start.9 = (s32[1,2]{1,0:T(1,128)S(1)}, s32[1,2]{1,0:T(1,128)}, u32[]{:S(2)}) copy-start(s32[1,2]{1,0:T(1,128)} %ids_ref.3) | copy-start | bytes 28

commit v4 on v3

--- a/solution.py
+++ b/solution.py
@@ -103,7 +103,8 @@
             return inputs[i].at[peer]
         return inputs[i].at[:, lanes(peer, held[i].shape[2])]
 
-    others = [lax.rem(me + step, peers) for step in range(1, peers)]
+    steps = sorted(range(1, peers), key=lambda step: abs(2 * step - peers))
+    others = [lax.rem(me + step, peers) for step in steps]
     barrier = pltpu.get_barrier_semaphore()
     for peer in others:
         pl.semaphore_signal(

time: 52.9 us -> 53.3 us (level)
  no operation moved by 1% of the time
where the time goes in v4:
time: 53.3 us; the launch traced here: 52.9 us
  Pallas kernels  42.1 us (79%)
  local copies, waits for them, and re-layouts  7.29 us (14%)
  matrix products  1.54 us (3%)
  other arithmetic  1.14 us (2%)
  between operations  0.83 us (2%)
    pallas_call x4, Pallas kernels, exchange(): pl.pallas_call(functools.partial(exchange_body, axis, cuts, joins), out_s...  35.1 us
    unnamed x28, local copies, waits for them, and re-layouts  6.11 us
    pallas_call x1, Pallas kernels, local(): pl.pallas_call(functools.partial(gather_tiles, own_blocks), out_shape=jax...  2.98 us
    pallas_call x1, Pallas kernels, local(): pl.pallas_call(functools.partial(scatter_tiles, own_blocks), out_shape=(j...  2.23 us
    pallas_call x1, Pallas kernels, local(): pl.pallas_call(add_hubs, out_shape=jax.ShapeDtypeStruct((columns, nodes),...  1.27 us

profile of v4, /device:TPU:0, one launch (start us, length us, event | category | flops | bytes accessed | tf_op | source)
XLA Modules:
  0.0 52.9 jit_solution(8806838991930571808)
XLA Ops:
  0.6 0.0 copy-start.13
  0.6 0.0 copy-start.2
  0.7 0.9 %copy-done.2 = bf16[16,4096]{1,0:T(8,128)(2,1)S(1)} copy-done((bf16[16,4096]{1,0:T(8,128)(2,1)S(1)}, bf16[16,4096]{1,0:T(8,128)(2,1)}, u32[]{:S(2)}) %copy-start.2) | copy-done | bytes 131096
  1.6 0.0 copy-start.8
  1.6 0.7 %copy-done.8 = s32[1,2]{1,0:T(1,128)S(1)} copy-done((s32[1,2]{1,0:T(1,128)S(1)}, s32[1,2]{1,0:T(1,128)}, u32[]{:S(2)}) %copy-start.8) | copy-done | bytes 32
  2.2 0.5 %pick_hubs.1.refs_0_ = bf16[16,256]{1,0:T(8,128)(2,1)S(1)} custom-call(s32[1,2]{1,0:T(1,128)S(1)} %copy-done.8, bf16[16,4096]{1,0:T(8,128)(2,1)S(1)} %copy-done.2), custom_call_target="tpu_custom_call" | custom-call | tf_op jit(solution)/shard_map/pick_hubs/pallas_call | solution.py:199
  2.8 4.7 %exchange_0.1.hubs_ref = bf16[16,1024]{1,0:T(8,128)(2,1)S(1)} custom-call(bf16[16,256]{1,0:T(8,128)(2,1)S(1)} %pick_hubs.1.refs_0_), custom_call_target="tpu_custom_call" | custom-call | tf_op jit(solution)/shard_map/exchange_0/pallas_call | solution.py:159
  7.5 0.9 %pad_maximum_fusion.1 = bf16[8,2,16,256]{3,2,1,0:T(8,128)(2,1)S(1)} fusion(bf16[8,1,16,256]{3,2,1,0:T(8,128)(2,1)} %bitcast.18, bf16[8,1,16,256]{3,2,1,0:T(8,128)(2,1)} %bitcast.19), kind=kLoop, calls=%fused_computation.8 | loop fusion | flops 65536 | bytes 262144 | tf_op jit(solution)/shard_map/stack | solution.py:220
  8.4 0.0 copy-start
  8.4 1.6 %copy-done = bf16[1,8,8,128,128]{4,3,2,1,0:T(8,128)(2,1)S(1)} copy-done((bf16[1,8,8,128,128]{4,3,2,1,0:T(8,128)(2,1)S(1)}, bf16[1,8,8,128,128]{4,3,2,1,0:T(8,128)(2,1)}, u32[]{:S(2)}) %copy-start) | copy-done | bytes 2097176
  10.0 0.0 copy-start.3
  10.0 0.9 %copy-done.3 = bf16[16,4096]{1,0:T(8,128)(2,1)S(1)} copy-done((bf16[16,4096]{1,0:T(8,128)(2,1)S(1)}, bf16[16,4096]{1,0:T(8,128)(2,1)}, u32[]{:S(2)}) %copy-start.3) | copy-done | bytes 131096
  10.9 0.0 copy-start.4
  10.9 0.7 %copy-done.4 = s32[1,8,8]{2,1,0:T(8,128)S(1)} copy-done((s32[1,8,8]{2,1,0:T(8,128)S(1)}, s32[1,8,8]{2,1,0:T(8,128)}, u32[]{:S(2)}) %copy-start.4) | copy-done | bytes 280
  11.6 0.0 copy-start.6
  11.6 0.7 %copy-done.6 = s32[1,8,8]{2,1,0:T(8,128)S(1)} copy-done((s32[1,8,8]{2,1,0:T(8,128)S(1)}, s32[1,8,8]{2,1,0:T(8,128)}, u32[]{:S(2)}) %copy-start.6) | copy-done | bytes 280
  12.3 0.0 copy-start.10
  12.3 0.7 %copy-done.10 = s32[1,8]{1,0:T(1,128)S(1)} copy-done((s32[1,8]{1,0:T(1,128)S(1)}, s32[1,8]{1,0:T(1,128)}, u32[]{:S(2)}) %copy-start.10) | copy-done | bytes 56
  12.9 3.0 %gather_tiles.1.refs_0_ = bf16[32,4096]{1,0:T(8,128)(2,1)S(1)} custom-call(s32[1,8,8]{2,1,0:T(8,128)S(1)} %copy-done.4, s32[1,8,8]{2,1,0:T(8,128)S(1)} %copy-done.6, s32[1,8]{1,0:T(1,128)S(1)} %copy-done.10, bf16[16,4096]{1,0:T(8,128)(2,1)S(1)} %copy-done.3, bf16[16,1024]{1,0:T(8,128)(2,1)S(1)} %exchange_0.1.hubs_ref, bf16[1,8,8,128,128]{4,3,2,1,0:T(8,128)(2,1)S(1)} %copy-done), custom_call_target="tpu_custom_call" | custom-call | tf_op jit(solution)/shard_map/gather_tiles/pallas_call | solution.py:209
  15.9 0.0 copy-start.12
  15.9 10.8 %exchange_1.1 = bf16[8,32,512]{2,1,0:T(8,128)(2,1)S(1)} custom-call(bf16[32,4096]{1,0:T(8,128)(2,1)S(1)} %gather_tiles.1.refs_0_), custom_call_target="tpu_custom_call" | custom-call | tf_op jit(solution)/shard_map/exchange_1/pallas_call | solution.py:159
  26.8 0.0 copy-done.13
  26.8 1.1 %multiply_convert_fusion.1 = (bf16[512,256]{1,0:T(8,128)(2,1)}, f32[512,256]{1,0:T(8,128)S(1)}) fusion(f32[256]{0:T(256)S(1)} %copy-done.13, bf16[256,512]{1,0:T(8,128)(2,1)S(1)} %bitcast.15, bf16[256,256]{1,0:T(8,128)(2,1)S(1)} %bitcast.16), kind=kOutput, calls=%fused_computation.4 | convolution fusion | flops 67895296 | bytes 1180672 | tf_op jit(solution)/shard_map/dot_general | solution.py:224
  27.8 0.0 copy-start.1
  27.8 0.0 copy-start.5
  27.8 0.0 copy-start.7
  27.8 0.0 copy-start.11
  27.8 0.0 copy-done.12
  27.8 0.2 fusion.1
  28.1 0.2 convolution_convert_fusion.1
  28.3 0.0 copy-start.9
  28.4 0.3 convolution_convert_fusion
  28.6 14.4 %exchange_2.1 = (bf16[32,4096]{1,0:T(8,128)(2,1)S(1)}, f32[48,256]{1,0:T(8,128)S(1)}) custom-call(bf16[8,32,512]{2,1,0:T(8,128)(2,1)S(1)} %bitcast.14, bf16[8,48,256]{2,1,0:T(8,128)(2,1)S(1)} %pad_maximum_fusion.refs_1_), custom_call_target="tpu_custom_call" | custom-call | tf_op jit(solution)/shard_map/exchange_2/pallas_call | solution.py:159
  43.0 0.0 copy-done.1
  43.0 0.0 copy-done.5
  43.1 0.0 copy-done.7
  43.1 0.0 copy-done.11
  43.1 2.2 %scatter_tiles.1 = (f32[16,4096]{1,0:T(8,128)S(1)}, bf16[16,1024]{1,0:T(8,128)(2,1)S(1)}) custom-call(s32[1,8,8]{2,1,0:T(8,128)S(1)} %copy-done.5, s32[1,8,8]{2,1,0:T(8,128)S(1)} %copy-done.7, s32[1,8]{1,0:T(1,128)S(1)} %copy-done.11, bf16[32,4096]{1,0:T(8,128)(2,1)S(1)} %get-tuple-element.11.g_ref, bf16[1,8,8,128,128]{4,3,2,1,0:T(8,128)(2,1)S(1)} %copy-done.1), custom_call_target="tpu_custom_call" | custom-call | tf_op jit(solution)/shard_map/scatter_tiles/pallas_call | solution.py:250
  45.3 5.2 %exchange_3.1 = (bf16[4,16,256]{2,1,0:T(8,128)(2,1)S(1)}, f32[48,256]{1,0:T(8,128)S(1)}) custom-call(bf16[16,1024]{1,0:T(8,128)(2,1)S(1)} %get-tuple-element.13.refs_0_, f32[48,256]{1,0:T(8,128)S(1)} %get-tuple-element.14.refs_1_), custom_call_target="tpu_custom_call" | custom-call | tf_op jit(solution)/shard_map/exchange_3/pallas_call | solution.py:159
  50.5 0.0 copy-done.9
  50.5 1.3 %add_hubs.1 = f32[16,4096]{1,0:T(8,128)} custom-call(s32[1,2]{1,0:T(1,128)S(1)} %copy-done.9, f32[16,4096]{1,0:T(8,128)S(1)} %get-tuple-element.12.part_ref, bf16[4,16,256]{2,1,0:T(8,128)(2,1)S(1)} %get-tuple-element.15.hub_ref), custom_call_target="tpu_custom_call" | custom-call | tf_op jit(solution)/shard_map/add_hubs/pallas_call | solution.py:263
  51.8 0.6 %slice.11 = f32[1,256]{1,0:T(1,128)} slice(f32[48,256]{1,0:T(8,128)S(1)} %get-tuple-element.16), slice={[32:33], [0:256]} | slice | bytes 2048 | tf_op jit(solution)/shard_map/slice | solution.py:276
  52.3 0.6 %fusion.2 = (f32[16,256]{1,0:T(8,128)}, f32[16,256]{1,0:T(8,128)}) fusion(f32[48,256]{1,0:T(8,128)S(1)} %get-tuple-element.16), kind=kLoop, calls=%fused_computation.10 | loop fusion | bytes 65536 | tf_op jit(solution)/shard_map/slice | solution.py:275
  (2 shorter events, 0.0 us)
Async XLA Ops:
  0.6 26.1 %copy-start.13 = (f32[256]{0:T(256)S(1)}, f32[256]{0:T(256)}, u32[]{:S(2)}) copy-start(f32[256]{0:T(256)} %param.13) | copy-start | bytes 3076
  0.6 0.9 %copy-start.2 = (bf16[16,4096]{1,0:T(8,128)(2,1)S(1)}, bf16[16,4096]{1,0:T(8,128)(2,1)}, u32[]{:S(2)}) copy-start(bf16[16,4096]{1,0:T(8,128)(2,1)} %features_ref.3) | copy-start | bytes 393220
  1.6 0.7 %copy-start.8 = (s32[1,2]{1,0:T(1,128)S(1)}, s32[1,2]{1,0:T(1,128)}, u32[]{:S(2)}) copy-start(s32[1,2]{1,0:T(1,128)} %ids_ref.3) | copy-start | bytes 28
  8.4 1.6 %copy-start = (bf16[1,8,8,128,128]{4,3,2,1,0:T(8,128)(2,1)S(1)}, bf16[1,8,8,128,128]{4,3,2,1,0:T(8,128)(2,1)}, u32[]{:S(2)}) copy-start(bf16[1,8,8,128,128]{4,3,2,1,0:T(8,128)(2,1)} %tiles_ref.3) | copy-start | bytes 6291460
  10.0 0.9 %copy-start.3 = (bf16[16,4096]{1,0:T(8,128)(2,1)S(1)}, bf16[16,4096]{1,0:T(8,128)(2,1)}, u32[]{:S(2)}) copy-start(bf16[16,4096]{1,0:T(8,128)(2,1)} %features_ref.3) | copy-start | bytes 393220
  10.9 0.7 %copy-start.4 = (s32[1,8,8]{2,1,0:T(8,128)S(1)}, s32[1,8,8]{2,1,0:T(8,128)}, u32[]{:S(2)}) copy-start(s32[1,8,8]{2,1,0:T(8,128)} %src_ref.3) | copy-start | bytes 772
  11.6 0.7 %copy-start.6 = (s32[1,8,8]{2,1,0:T(8,128)S(1)}, s32[1,8,8]{2,1,0:T(8,128)}, u32[]{:S(2)}) copy-start(s32[1,8,8]{2,1,0:T(8,128)} %dst_ref.3) | copy-start | bytes 772
  12.3 0.7 %copy-start.10 = (s32[1,8]{1,0:T(1,128)S(1)}, s32[1,8]{1,0:T(1,128)}, u32[]{:S(2)}) copy-start(s32[1,8]{1,0:T(1,128)} %count_ref.3) | copy-start | bytes 100
  15.9 11.9 %copy-start.12 = (bf16[512,256]{1,0:T(8,128)(2,1)S(1)}, bf16[512,256]{1,0:T(8,128)(2,1)}, u32[]{:S(2)}) copy-start(bf16[512,256]{1,0:T(8,128)(2,1)} %param.19) | copy-start | bytes 786436
  27.8 15.2 %copy-start.1 = (bf16[1,8,8,128,128]{4,3,2,1,0:T(8,128)(2,1)S(1)}, bf16[1,8,8,128,128]{4,3,2,1,0:T(8,128)(2,1)}, u32[]{:S(2)}) copy-start(bf16[1,8,8,128,128]{4,3,2,1,0:T(8,128)(2,1)} %tiles_ref.3) | copy-start | bytes 6291460
  27.8 15.2 %copy-start.5 = (s32[1,8,8]{2,1,0:T(8,128)S(1)}, s32[1,8,8]{2,1,0:T(8,128)}, u32[]{:S(2)}) copy-start(s32[1,8,8]{2,1,0:T(8,128)} %src_ref.3) | copy-start | bytes 772
  27.8 15.2 %copy-start.7 = (s32[1,8,8]{2,1,0:T(8,128)S(1)}, s32[1,8,8]{2,1,0:T(8,128)}, u32[]{:S(2)}) copy-start(s32[1,8,8]{2,1,0:T(8,128)} %dst_ref.3) | copy-start | bytes 772
  27.8 15.2 %copy-start.11 = (s32[1,8]{1,0:T(1,128)S(1)}, s32[1,8]{1,0:T(1,128)}, u32[]{:S(2)}) copy-start(s32[1,8]{1,0:T(1,128)} %count_ref.3) | copy-start | bytes 100
  28.3 22.2 %copy-start.9 = (s32[1,2]{1,0:T(1,128)S(1)}, s32[1,2]{1,0:T(1,128)}, u32[]{:S(2)}) copy-start(s32[1,2]{1,0:T(1,128)} %ids_ref.3) | copy-start | bytes 28
